TPU v7x, 32 devices: a whole 2x2x4 slice. The times are simulated.
32 devices in a mesh: ens: 4 (over y, x), lat: 8 (over z, core).
Axes of the slice: x: 2, y: 2, z: 4, core: 2. Of those that a mesh axis runs over, the one named last changes fastest.
Arguments:
- prediction_array: float32 [16, 16, 64, 1440], P('ens', None, 'lat'), may hold values from -6 to 6
- verifying_analysis: float32 [16, 64, 1440], P('ens', 'lat'), may hold values from -6 to 6
- variable_penalty_factor: float32 [16], replicated, may hold values from 0.25 to 4
Outputs:
- field_grad: float32 [16, 16, 64, 1440], P('ens', None, 'lat')
All inputs are finite; a program needn't handle non-finite values.
Results may differ from a plain program's by a relative error of at most 0.00002.
Values sent between devices are 32-bit elements; how exact they have to be, the bound alone decides.
A program may use at most 64 MiB of HBM per device.

v0:
```python
import jax
import jax.numpy as jnp
from jax import lax
from jax.sharding import PartitionSpec as P

COARSE = 3


def with_halo(block, sides, width):
    for axis, dim in sides:
        count = lax.axis_size(axis)
        forward = [(i, i + 1) for i in range(count - 1)]
        backward = [(target, source) for source, target in forward]
        low = lax.ppermute(
            lax.slice_in_dim(block, block.shape[dim] - width, None, axis=dim), axis, forward
        )
        high = lax.ppermute(lax.slice_in_dim(block, 0, width, axis=dim), axis, backward)
        block = jnp.concatenate([low, block, high], axis=dim)
    return block


def slope(differ):
    return differ * lax.rsqrt(differ * differ + 0.01)


def normal_kernel_smoother(extended, first_row, lat_total):
    along = 0.25 * extended[:, :-2] + 0.5 * extended[:, 1:-1] + 0.25 * extended[:, 2:]
    result = 0.25 * jnp.roll(along, 1, -1) + 0.5 * along + 0.25 * jnp.roll(along, -1, -1)
    row_ids = first_row + 1 + jnp.arange(result.shape[1])
    inside = (row_ids >= 0) & (row_ids < lat_total)
    return jnp.where(inside[None, :, None], result, 0.0)


def near_forward(field, lat_start, lat_total):
    extended = with_halo(field, (("lat", 1),), 1)
    return normal_kernel_smoother(extended, lat_start - 1, lat_total)


def near_back(field, lat_start, lat_total):
    extended = with_halo(field, (("lat", 1),), 1)
    return normal_kernel_smoother(extended, lat_start - 1, lat_total)


def forward_blur(stacked_fields, lat_start, lat_total):
    fine_part = near_forward(stacked_fields, lat_start, lat_total)
    level = fine_part
    for repeat in range(COARSE - 1):
        level = near_forward(level, lat_start, lat_total)
    return (fine_part, level)


def back_blur(fine_grad, coarse_grad, lat_start, lat_total):
    level = coarse_grad
    for repeat in range(COARSE - 1):
        level = near_back(level, lat_start, lat_total)
    level = level + fine_grad
    return near_back(level, lat_start, lat_total)


def couple_derivative(smooth_fc, smooth_obs, penalty_factor):
    count = smooth_fc.shape[0]

    def single(member):
        return jnp.sum(slope(member[None] - smooth_fc), axis=0)

    pulls = lax.map(single, smooth_fc)
    return penalty_factor * (slope(smooth_fc - smooth_obs[None]) - 0.95 / (count - 1) * pulls)


def body(prediction_array, verifying_analysis, variable_penalty_factor):
    ensemble_size, variable_number, parallel_number, meridian_number = prediction_array.shape
    group_size = verifying_analysis.shape[0]
    ens_index = lax.axis_index("ens")
    lat_start = lax.axis_index("lat") * parallel_number
    lat_total = lax.axis_size("lat") * parallel_number
    row_ids = (lat_start + jnp.arange(parallel_number)).astype(jnp.float32)
    degrees = 0.25 * (row_ids - (lat_total - 1) / 2.0)
    lat_weight = jnp.cos(jnp.deg2rad(degrees))
    chan_weight = lax.dynamic_slice_in_dim(
        variable_penalty_factor, ens_index * group_size, group_size
    )
    penalty_factor = chan_weight[:, None, None] * lat_weight[None, :, None]
    regrouped = lax.all_to_all(prediction_array, "ens", split_axis=1, concat_axis=0, tiled=True)
    all_members = regrouped.shape[0]
    divide_parallels = all_members * group_size
    stacked_fields = jnp.concatenate(
        [regrouped.reshape(divide_parallels, parallel_number, meridian_number), verifying_analysis],
        0,
    )
    fine_all, coarse_all = forward_blur(stacked_fields, lat_start, lat_total)
    fine_group = fine_all[:divide_parallels].reshape(
        all_members, group_size, parallel_number, meridian_number
    )
    coarse_group = coarse_all[:divide_parallels].reshape(
        all_members, group_size, parallel_number, meridian_number
    )
    sharp_derivative = couple_derivative(fine_group, fine_all[divide_parallels:], penalty_factor)
    grad_coarse = couple_derivative(coarse_group, coarse_all[divide_parallels:], penalty_factor)
    combined = back_blur(
        sharp_derivative.reshape(divide_parallels, parallel_number, meridian_number),
        grad_coarse.reshape(divide_parallels, parallel_number, meridian_number),
        lat_start,
        lat_total,
    )
    return lax.all_to_all(
        combined.reshape(all_members, group_size, parallel_number, meridian_number),
        "ens",
        split_axis=0,
        concat_axis=1,
        tiled=True,
    )


def solution(mesh):
    placed = (P("ens", None, "lat", None), P("ens", "lat", None), P())
    return jax.shard_map(
        body, mesh=mesh, in_specs=placed, out_specs=P("ens", None, "lat", None), check_vma=False
    )
```

profile of v0, /device:TPU:11, one launch (start us, length us, event | category | flops | bytes accessed | tf_op | source)
XLA Modules:
  0.0 298.6 jit_solution(8236508981447693382)
XLA Ops:
  0.0 2.1 copy.12
  2.1 38.4 %all_to_all.33 = f32[4,16,8,1440]{3,2,0,1:T(8,128)S(1)} all-to-all(f32[4,16,8,1440]{3,2,0,1:T(8,128)S(1)} %copy.12), channel_id=1, replica_groups=mesh['ens'=4,'lat'=8] {'ens'}, dimensions={1} | all-to-all | bytes 5898240 | tf_op jit(solution)/shard_map/all_to_all | solution.py:83
  41.4 1.4 fusion.44
  42.7 4.9 %collective-permute-start = (f32[68,1,1440]{2,1,0:T(1,128)}, f32[68,1,1440]{2,1,0:T(1,128)}, u32[]{:S(2)}, u32[]{:S(2)}) collective-permute-start(f32[68,1,1440]{2,1,0:T(1,128)} %get-tuple-element.69), channel_id=1, source_target_pairs={{0,1},{1,2},{2,3},{3,4},{4,5},{5,6},{6,7},{8,9},{9,10},{10,11},{11... | collective-permute-start | bytes 1175048 | tf_op jit(solution)/shard_map/ppermute | solution.py:14
  47.7 1.9 collective-permute-start.1
  49.7 3.3 %collective-permute-done = f32[68,1,1440]{2,1,0:T(1,128)} collective-permute-done((f32[68,1,1440]{2,1,0:T(1,128)}, f32[68,1,1440]{2,1,0:T(1,128)}, u32[]{:S(2)}, u32[]{:S(2)}) %collective-permute-start) | collective-permute-done | bytes 391712 | tf_op jit(solution)/shard_map/ppermute | solution.py:14
  53.0 4.4 %collective-permute-done.1 = f32[68,1,1440]{2,1,0:T(1,128)} collective-permute-done((f32[68,1,1440]{2,1,0:T(1,128)}, f32[68,1,1440]{2,1,0:T(1,128)}, u32[]{:S(2)}, u32[]{:S(2)}) %collective-permute-start.1) | collective-permute-done | bytes 391712 | tf_op jit(solution)/shard_map/ppermute | solution.py:17
  57.4 3.2 %fusion.2 = f32[68,8,1440]{2,1,0:T(8,128)S(1)} fusion(f32[4,8,1440]{2,1,0:T(8,128)S(1)} %copy-done.6, f32[68,1,1440]{2,1,0:T(1,128)} %collective-permute-done.1, f32[64,8,1440]{2,1,0:T(8,128)S(1)} %bitcast.36, f32[68,1,1440]{2,1,0:T(1,128)} %collective-permute-done), kind=kLoop, calls=%fused_computation.11 | loop fusion | flops 7833600 | bytes 7050240 | tf_op jit(solution)/shard_map/add | solution.py:27
  62.1 1.3 fusion.15
  63.4 1.8 fusion.51
  65.2 1.9 collective-permute-start.2
  67.1 2.4 collective-permute-start.3
  69.7 2.7 collective-permute-done.2
  72.4 4.4 %collective-permute-done.3 = f32[68,1,1440]{2,1,0:T(1,128)} collective-permute-done((f32[68,1,1440]{2,1,0:T(1,128)}, f32[68,1,1440]{2,1,0:T(1,128)}, u32[]{:S(2)}, u32[]{:S(2)}) %collective-permute-start.3) | collective-permute-done | bytes 391712 | tf_op jit(solution)/shard_map/ppermute | solution.py:17
  76.8 2.8 fusion.8
  81.0 3.9 %fusion.18 = f32[68,8,1440]{2,1,0:T(8,128)S(1)} fusion(f32[68,8,1439]{2,1,0:T(8,128)S(1)} %get-tuple-element.60, f32[68,8,1]{2,1,0:T(8,128)S(1)} %get-tuple-element.62, f32[68,8,1]{2,1,0:T(8,128)S(1)} %get-tuple-element.61, f32[68,8,1439]{2,1,0:T(8,128)S(1)} %get-tuple-element.59, pred[8]{0:T(512)(128)(4,1)S(1)} %compare_and_fusion, ...), kind=kLoop, calls=%fused_computation.38 | loop fusion | flops 11750400 | bytes 13317128 | tf_op jit(solution)/shard_map/jit(_where)/select_n | solution.py:31
  84.9 1.7 copy-done.3
  86.7 1.4 fusion.48
  88.1 1.9 collective-permute-start.4
  90.0 2.6 collective-permute-start.5
  92.6 2.1 broadcast.99.clone
  94.6 21.6 %while.21 = (s32[]{:T(128)}, f32[16,4,8,1440]{3,2,1,0:T(8,128)}, f32[16,4,8,1440]{3,2,1,0:T(8,128)S(1)}, s32[]{:T(128)}) while((s32[]{:T(128)}, f32[16,4,8,1440]{3,2,1,0:T(8,128)}, f32[16,4,8,1440]{3,2,1,0:T(8,128)S(1)}, s32[]{:T(128)}) %tuple.56), condition=%wide.region_5.6_spmd, body=%wide.region_3.5_spmd.sunk | while | flops 3640322 | bytes 4067897 | solution.py:66
  116.2 6.8 %fusion.4 = f32[68,8,1440]{2,1,0:T(8,128)S(1)} fusion(f32[68,1,1440]{2,1,0:T(1,128)} %collective-permute-done.5, f32[68,8,1440]{2,1,0:T(8,128)} %copy-done.3, f32[68,1,1440]{2,1,0:T(1,128)} %collective-permute-done.4), kind=kLoop, calls=%fused_computation.14 | loop fusion | flops 5483520 | bytes 7050240 | tf_op jit(solution)/shard_map/add | solution.py:27
  125.0 4.0 %fusion.21 = f32[68,8,1440]{2,1,0:T(8,128)S(1)} fusion(f32[68,8,1439]{2,1,0:T(8,128)S(1)} %get-tuple-element.54, f32[68,8,1]{2,1,0:T(8,128)S(1)} %get-tuple-element.56, f32[68,8,1]{2,1,0:T(8,128)S(1)} %get-tuple-element.55, f32[68,8,1439]{2,1,0:T(8,128)S(1)} %get-tuple-element.53, pred[8]{0:T(512)(128)(4,1)S(1)} %compare_and_fusion, ...), kind=kLoop, calls=%fused_computation.43 | loop fusion | flops 11750400 | bytes 13317128 | tf_op jit(solution)/shard_map/jit(_where)/select_n | solution.py:31
  129.0 2.1 slice.248
  131.7 2.0 broadcast.99.clone.1
  133.7 66.9 %while.20 = (s32[]{:T(128)}, f32[16,4,8,1440]{3,2,1,0:T(8,128)}, f32[16,4,8,1440]{3,2,1,0:T(8,128)}, s32[]{:T(128)}) while((s32[]{:T(128)}, f32[16,4,8,1440]{3,2,1,0:T(8,128)}, f32[16,4,8,1440]{3,2,1,0:T(8,128)}, s32[]{:T(128)}) %tuple.57), condition=%wide.region_2.3_spmd, body=%wide.region_0.2_spmd.sunk | while | flops 3640322 | bytes 4067897 | solution.py:66
  134.8 2.6 multiply_reduce_fusion.4
  139.0 2.5 multiply_reduce_fusion.4
  143.2 2.5 multiply_reduce_fusion.4
  147.4 2.5 multiply_reduce_fusion.4
  151.5 2.5 multiply_reduce_fusion.4
  155.7 2.5 multiply_reduce_fusion.4
  159.9 2.5 multiply_reduce_fusion.4
  164.0 2.5 multiply_reduce_fusion.4
  168.2 2.5 multiply_reduce_fusion.4
  172.4 2.5 multiply_reduce_fusion.4
  176.6 2.5 multiply_reduce_fusion.4
  180.7 2.5 multiply_reduce_fusion.4
  184.9 2.5 multiply_reduce_fusion.4
  189.1 2.5 multiply_reduce_fusion.4
  193.2 2.5 multiply_reduce_fusion.4
  197.4 2.5 multiply_reduce_fusion.4
  200.7 4.6 %subtract_multiply_fusion = (f32[16,4,8,1440]{3,2,1,0:T(8,128)S(1)}, f32[16,4,8,1440]{3,2,1,0:T(8,128)S(1)}) fusion(f32[16,4,8,1440]{3,2,1,0:T(8,128)} %get-tuple-element.40, f32[16,4,8,1440]{3,2,1,0:T(8,128)S(1)} %copy-done.2, f32[4,8,1440]{2,1,0:T(8,128)S(1)} %slice-done.1, f32[4,8]{1,0:T(4,128)S(1)} %broadcast_multiply_fusion, ...), kind=kLoop, calls=%fused_computation.79 | loop fusion | flops 10321920 | bytes 18063488 | tf_op jit(solution)/shard_map/mul | solution.py:67
  205.8 3.2 %collective-permute-start.6 = (f32[64,1,1440]{2,1,0:T(1,128)S(1)}, f32[64,1,1440]{2,1,0:T(1,128)S(1)}, u32[]{:S(2)}, u32[]{:S(2)}) collective-permute-start(f32[64,1,1440]{2,1,0:T(1,128)S(1)} %get-tuple-element.87), channel_id=1, source_target_pairs={{0,1},{1,2},{2,3},{3,4},{4,5},{5,6},{6,7},{8,9},{9,10},{10,11},{11... | collective-permute-start | bytes 1105928 | tf_op jit(solution)/shard_map/ppermute | solution.py:14
  209.0 2.1 collective-permute-start.7
  211.1 2.6 collective-permute-done.6
  213.7 4.4 %collective-permute-done.7 = f32[64,1,1440]{2,1,0:T(1,128)S(1)} collective-permute-done((f32[64,1,1440]{2,1,0:T(1,128)S(1)}, f32[64,1,1440]{2,1,0:T(1,128)S(1)}, u32[]{:S(2)}, u32[]{:S(2)}) %collective-permute-start.7) | collective-permute-done | bytes 368672 | tf_op jit(solution)/shard_map/ppermute | solution.py:17
  218.1 1.5 fusion.31
  221.0 2.7 fusion.36
  224.2 1.9 collective-permute-start.8
  226.1 2.4 collective-permute-start.9
  228.5 2.3 collective-permute-done.8
  230.8 4.4 %collective-permute-done.9 = f32[64,1,1440]{2,1,0:T(1,128)S(1)} collective-permute-done((f32[64,1,1440]{2,1,0:T(1,128)S(1)}, f32[64,1,1440]{2,1,0:T(1,128)S(1)}, u32[]{:S(2)}, u32[]{:S(2)}) %collective-permute-start.9) | collective-permute-done | bytes 368672 | tf_op jit(solution)/shard_map/ppermute | solution.py:17
  235.2 1.5 fusion.27
  238.1 3.0 %fusion.40 = f32[64,8,1440]{2,1,0:T(8,128)S(1)} fusion(f32[64,8,1439]{2,1,0:T(8,128)S(1)} %get-tuple-element.78, f32[64,8,1]{2,1,0:T(8,128)S(1)} %get-tuple-element.80, f32[64,8,1]{2,1,0:T(8,128)S(1)} %get-tuple-element.79, f32[64,8,1439]{2,1,0:T(8,128)S(1)} %get-tuple-element.77, f32[16,4,8,1440]{3,2,1,0:T(8,128)S(1)} %get-tuple-element.89, ...), kind=kLoop, calls=%fused_computation.72 | loop fusion | flops 11796480 | bytes 15482888 | tf_op jit(solution)/shard_map/add | solution.py:56
  241.6 1.9 collective-permute-start.10
  243.6 2.7 collective-permute-start.11
  246.2 2.0 collective-permute-done.10
  248.3 4.4 %collective-permute-done.11 = f32[64,1,1440]{2,1,0:T(1,128)S(1)} collective-permute-done((f32[64,1,1440]{2,1,0:T(1,128)S(1)}, f32[64,1,1440]{2,1,0:T(1,128)S(1)}, u32[]{:S(2)}, u32[]{:S(2)}) %collective-permute-start.11) | collective-permute-done | bytes 368672 | tf_op jit(solution)/shard_map/ppermute | solution.py:17
  252.6 1.5 fusion.23
  255.6 2.7 fusion.43
  258.3 38.5 %all_to_all.34 = f32[16,4,8,1440]{3,2,1,0:T(8,128)S(1)} all-to-all(f32[16,4,8,1440]{3,2,1,0:T(8,128)S(1)} %bitcast.39), channel_id=1, replica_groups=mesh['ens'=4,'lat'=8] {'ens'}, dimensions={0} | all-to-all | bytes 5898240 | tf_op jit(solution)/shard_map/all_to_all | solution.py:105
  296.8 1.9 copy.15
  (123 shorter events, 59.9 us)
Async XLA Ops:
  40.5 0.9 copy-start.6
  42.7 10.2 %collective-permute-start = (f32[68,1,1440]{2,1,0:T(1,128)}, f32[68,1,1440]{2,1,0:T(1,128)}, u32[]{:S(2)}, u32[]{:S(2)}) collective-permute-start(f32[68,1,1440]{2,1,0:T(1,128)} %get-tuple-element.69), channel_id=1, source_target_pairs={{0,1},{1,2},{2,3},{3,4},{4,5},{5,6},{6,7},{8,9},{9,10},{10,11},{11... | collective-permute-start | bytes 1175048 | tf_op jit(solution)/shard_map/ppermute | solution.py:14
  47.7 9.7 %collective-permute-start.1 = (f32[68,1,1440]{2,1,0:T(1,128)}, f32[68,1,1440]{2,1,0:T(1,128)}, u32[]{:S(2)}, u32[]{:S(2)}) collective-permute-start(f32[68,1,1440]{2,1,0:T(1,128)} %get-tuple-element.70), channel_id=1, source_target_pairs={{1,0},{2,1},{3,2},{4,3},{5,4},{6,5},{7,6},{9,8},{10,9},{11,10},{12... | collective-permute-start | bytes 1175048 | tf_op jit(solution)/shard_map/ppermute | solution.py:17
  62.1 7.4 %copy-start.7 = (f32[16]{0:T(128)S(1)}, f32[16]{0:T(128)}, u32[]{:S(2)}) copy-start(f32[16]{0:T(128)} %param.9) | copy-start | bytes 196
  63.4 17.6 %copy-start = (f32[68,8,1440]{2,1,0:T(8,128)}, f32[68,8,1440]{2,1,0:T(8,128)S(1)}, u32[]{:S(2)}) copy-start(f32[68,8,1440]{2,1,0:T(8,128)S(1)} %fusion.15) | copy-start | bytes 9400324
  65.2 7.2 %collective-permute-start.2 = (f32[68,1,1440]{2,1,0:T(1,128)}, f32[68,1,1440]{2,1,0:T(1,128)}, u32[]{:S(2)}, u32[]{:S(2)}) collective-permute-start(f32[68,1,1440]{2,1,0:T(1,128)} %get-tuple-element.63), channel_id=1, source_target_pairs={{0,1},{1,2},{2,3},{3,4},{4,5},{5,6},{6,7},{8,9},{9,10},{10,11},{11... | collective-permute-start | bytes 1175048 | tf_op jit(solution)/shard_map/ppermute | solution.py:14
  67.1 9.7 %collective-permute-start.3 = (f32[68,1,1440]{2,1,0:T(1,128)}, f32[68,1,1440]{2,1,0:T(1,128)}, u32[]{:S(2)}, u32[]{:S(2)}) collective-permute-start(f32[68,1,1440]{2,1,0:T(1,128)} %get-tuple-element.64), channel_id=1, source_target_pairs={{1,0},{2,1},{3,2},{4,3},{5,4},{6,5},{7,6},{9,8},{10,9},{11,10},{12... | collective-permute-start | bytes 1175048 | tf_op jit(solution)/shard_map/ppermute | solution.py:17
  84.9 1.7 copy-start.3
  86.7 8.0 %slice-start = ((f32[68,8,1440]{2,1,0:T(8,128)}), f32[64,8,1440]{2,1,0:T(8,128)S(1)}, s32[]{:S(2)}) async-start(f32[68,8,1440]{2,1,0:T(8,128)} %copy-done), calls=%async_computation.2 | async-start | bytes 6291456 | tf_op jit(solution)/shard_map/slice | solution.py:91
  88.1 28.1 %collective-permute-start.4 = (f32[68,1,1440]{2,1,0:T(1,128)}, f32[68,1,1440]{2,1,0:T(1,128)}, u32[]{:S(2)}, u32[]{:S(2)}) collective-permute-start(f32[68,1,1440]{2,1,0:T(1,128)} %get-tuple-element.57), channel_id=1, source_target_pairs={{0,1},{1,2},{2,3},{3,4},{4,5},{5,6},{6,7},{8,9},{9,10},{10,11},{11... | collective-permute-start | bytes 1175048 | tf_op jit(solution)/shard_map/ppermute | solution.py:14
  90.0 26.2 %collective-permute-start.5 = (f32[68,1,1440]{2,1,0:T(1,128)}, f32[68,1,1440]{2,1,0:T(1,128)}, u32[]{:S(2)}, u32[]{:S(2)}) collective-permute-start(f32[68,1,1440]{2,1,0:T(1,128)} %get-tuple-element.58), channel_id=1, source_target_pairs={{1,0},{2,1},{3,2},{4,3},{5,4},{6,5},{7,6},{9,8},{10,9},{11,10},{12... | collective-permute-start | bytes 1175048 | tf_op jit(solution)/shard_map/ppermute | solution.py:17
  116.2 6.8 %copy-start.1 = (f32[16,4,8,1440]{3,2,1,0:T(8,128)}, f32[16,4,8,1440]{3,2,1,0:T(8,128)S(1)}, u32[]{:S(2)}) copy-start(f32[16,4,8,1440]{3,2,1,0:T(8,128)S(1)} %get-tuple-element.153) | copy-start | bytes 8847364
  123.0 1.9 copy-start.4
  129.0 2.7 copy-start.5
  133.7 66.9 %copy-start.2 = (f32[16,4,8,1440]{3,2,1,0:T(8,128)S(1)}, f32[16,4,8,1440]{3,2,1,0:T(8,128)}, u32[]{:S(2)}) copy-start(f32[16,4,8,1440]{3,2,1,0:T(8,128)} %copy-done.1) | copy-start | bytes 8847364
  133.7 66.9 %slice-start.1 = ((f32[68,8,1440]{2,1,0:T(8,128)}), f32[4,8,1440]{2,1,0:T(8,128)S(1)}, s32[]{:S(2)}) async-start(f32[68,8,1440]{2,1,0:T(8,128)} %copy-done), calls=%async_computation.3 | async-start | bytes 393216 | tf_op jit(solution)/shard_map/slice | solution.py:97
  133.7 66.9 %slice-start.2 = ((f32[68,8,1440]{2,1,0:T(8,128)}), f32[4,8,1440]{2,1,0:T(8,128)S(1)}, s32[]{:S(2)}) async-start(f32[68,8,1440]{2,1,0:T(8,128)} %copy-done.5), calls=%async_computation.4 | async-start | bytes 393216 | tf_op jit(solution)/shard_map/slice | solution.py:98
  205.8 7.9 %collective-permute-start.6 = (f32[64,1,1440]{2,1,0:T(1,128)S(1)}, f32[64,1,1440]{2,1,0:T(1,128)S(1)}, u32[]{:S(2)}, u32[]{:S(2)}) collective-permute-start(f32[64,1,1440]{2,1,0:T(1,128)S(1)} %get-tuple-element.87), channel_id=1, source_target_pairs={{0,1},{1,2},{2,3},{3,4},{4,5},{5,6},{6,7},{8,9},{9,10},{10,11},{11... | collective-permute-start | bytes 1105928 | tf_op jit(solution)/shard_map/ppermute | solution.py:14
  209.0 9.1 %collective-permute-start.7 = (f32[64,1,1440]{2,1,0:T(1,128)S(1)}, f32[64,1,1440]{2,1,0:T(1,128)S(1)}, u32[]{:S(2)}, u32[]{:S(2)}) collective-permute-start(f32[64,1,1440]{2,1,0:T(1,128)S(1)} %get-tuple-element.88), channel_id=1, source_target_pairs={{1,0},{2,1},{3,2},{4,3},{5,4},{6,5},{7,6},{9,8},{10,9},{11,10},{12... | collective-permute-start | bytes 1105928 | tf_op jit(solution)/shard_map/ppermute | solution.py:17
  224.2 6.6 %collective-permute-start.8 = (f32[64,1,1440]{2,1,0:T(1,128)S(1)}, f32[64,1,1440]{2,1,0:T(1,128)S(1)}, u32[]{:S(2)}, u32[]{:S(2)}) collective-permute-start(f32[64,1,1440]{2,1,0:T(1,128)S(1)} %get-tuple-element.81), channel_id=1, source_target_pairs={{0,1},{1,2},{2,3},{3,4},{4,5},{5,6},{6,7},{8,9},{9,10},{10,11},{11... | collective-permute-start | bytes 1105928 | tf_op jit(solution)/shard_map/ppermute | solution.py:14
  226.1 9.1 %collective-permute-start.9 = (f32[64,1,1440]{2,1,0:T(1,128)S(1)}, f32[64,1,1440]{2,1,0:T(1,128)S(1)}, u32[]{:S(2)}, u32[]{:S(2)}) collective-permute-start(f32[64,1,1440]{2,1,0:T(1,128)S(1)} %get-tuple-element.82), channel_id=1, source_target_pairs={{1,0},{2,1},{3,2},{4,3},{5,4},{6,5},{7,6},{9,8},{10,9},{11,10},{12... | collective-permute-start | bytes 1105928 | tf_op jit(solution)/shard_map/ppermute | solution.py:17
  241.6 6.6 %collective-permute-start.10 = (f32[64,1,1440]{2,1,0:T(1,128)S(1)}, f32[64,1,1440]{2,1,0:T(1,128)S(1)}, u32[]{:S(2)}, u32[]{:S(2)}) collective-permute-start(f32[64,1,1440]{2,1,0:T(1,128)S(1)} %get-tuple-element.75), channel_id=1, source_target_pairs={{0,1},{1,2},{2,3},{3,4},{4,5},{5,6},{6,7},{8,9},{9,10},{10,11},{11... | collective-permute-start | bytes 1105928 | tf_op jit(solution)/shard_map/ppermute | solution.py:14
  243.6 9.1 %collective-permute-start.11 = (f32[64,1,1440]{2,1,0:T(1,128)S(1)}, f32[64,1,1440]{2,1,0:T(1,128)S(1)}, u32[]{:S(2)}, u32[]{:S(2)}) collective-permute-start(f32[64,1,1440]{2,1,0:T(1,128)S(1)} %get-tuple-element.76), channel_id=1, source_target_pairs={{1,0},{2,1},{3,2},{4,3},{5,4},{6,5},{7,6},{9,8},{10,9},{11,10},{12... | collective-permute-start | bytes 1105928 | tf_op jit(solution)/shard_map/ppermute | solution.py:17
where the time goes:
time: 301 us; the launch traced here: 299 us
  other arithmetic  91.8 us (30%)
  blocking collectives  76.9 us (26%)
  local copies, waits for them, and re-layouts  64.7 us (21%)
  waiting for transfers between devices  34.8 us (12%)
  starting transfers between devices  29.9 us (10%)
    reduce_sum x32, other arithmetic, single(): return jnp.sum(slope(member[None] - smooth_fc), axis=0)  50.6 us
    all_to_all x1, blocking collectives, body(): lax.all_to_all(combined.reshape(all_members, group_size, parallel_number,...  38.5 us
    all_to_all x1, blocking collectives, body(): lax.all_to_all(prediction_array, 'ens', split_axis=1, concat_axis=0, tile...  38.4 us
    dynamic_update_slice x32, local copies, waits for them, and re-layouts, couple_derivative(): pulls = lax.map(single, smooth_fc)  22.3 us
    ppermute x6, waiting for transfers between devices, with_halo(): lax.ppermute(lax.slice_in_dim(block, 0, width, axis=dim), axis, backward)  22 us
    add x6, other arithmetic, normal_kernel_smoother(): 0.25 * extended[:, :-2] + 0.5 * extended[:, 1:-1] + 0.25 * extended[:, 2:]  17.5 us
    ppermute x6, starting transfers between devices, with_halo(): lax.ppermute(lax.slice_in_dim(block, block.shape[dim] - width, None, axis...  15.8 us
    sub x32, local copies, waits for them, and re-layouts, single(): return jnp.sum(slope(member[None] - smooth_fc), axis=0)  15.4 us
  transfers between devices with their start and end apart: 12, of which 10 were waited for; matrix products, arithmetic and copies ran while one was open for 8% of the time, Pallas kernels for 0%

commit v1 on v0

v1 whole, which is shorter than its diff:
```python
import functools

import jax
import jax.numpy as jnp
import numpy as np
from jax import lax
from jax.experimental import pallas as pl
from jax.experimental.pallas import tpu as pltpu
from jax.sharding import PartitionSpec as P

COARSE = 3
LANES = 128
MESH = pl.DeviceIdType.MESH


def round_up(value, unit):
    return -(-value // unit) * unit


def band_matrices(fields, rows):
    half = rows // 2
    pairs = fields // 2
    out = np.zeros((4, 2 * fields * rows, 2 * fields * rows), np.float32)
    window = 2 * rows
    band = 0.5 * np.eye(window) + 0.25 * np.eye(window, k=1) + 0.25 * np.eye(window, k=-1)
    places = np.arange(window) - half
    for variant in range(4):
        keep = np.ones(window)
        if variant & 1:
            keep[places < 0] = 0.0
        if variant & 2:
            keep[places >= rows] = 0.0
        step = keep[:, None] * band * keep[None, :]
        scales = (step, np.linalg.matrix_power(step, COARSE))
        for scale, matrix in enumerate(scales):
            matrix = matrix[half : half + rows]
            for field in range(fields):
                at = (scale * fields + field) * rows
                out[variant, at : at + rows, field * rows : (field + 1) * rows] = matrix[:, half : half + rows]
                tile, part = field % pairs, field // pairs
                low = (fields + tile) * rows + part * half
                out[variant, at : at + rows, low : low + half] = matrix[:, :half]
                high = (fields + pairs + tile) * rows + part * half
                out[variant, at : at + rows, high : high + half] = matrix[:, half + rows :]
    return out


def split_dot(matrix, values):
    first = values.astype(jnp.bfloat16)
    rest = values - first.astype(jnp.float32)
    second = rest.astype(jnp.bfloat16)
    third = (rest - second.astype(jnp.float32)).astype(jnp.bfloat16)
    total = jnp.dot(matrix, third, preferred_element_type=jnp.float32)
    total = total + jnp.dot(matrix, second, preferred_element_type=jnp.float32)
    return total + jnp.dot(matrix, first, preferred_element_type=jnp.float32)


def wrapped(tiles, width):
    whole = width // LANES
    rest = width - whole * LANES
    last = tiles[:, whole * LANES :]
    lane = lax.broadcasted_iota(jnp.int32, last.shape, 1)
    ahead = pltpu.roll(tiles[:, :LANES], rest, 1)
    behind = pltpu.roll(last, LANES - rest, 1)
    last = jnp.where(lane < rest, last, jnp.where(lane < (LANES + rest) // 2, ahead, behind))
    return jnp.concatenate([tiles[:, : whole * LANES], last], axis=1)


def lon_pass(tiles):
    size = tiles.shape[1]
    return 0.25 * (pltpu.roll(tiles, 1, 1) + pltpu.roll(tiles, size - 1, 1)) + 0.5 * tiles


def lon_blur(ref, count, width):
    def step(field, carry):
        ref[field] = lon_pass(wrapped(ref[field], width))
        coarse = wrapped(ref[count + field], width)
        for _ in range(COARSE):
            coarse = lon_pass(coarse)
        ref[count + field] = coarse
        return carry

    lax.fori_loop(0, count, step, 0)


def slope(differ):
    return differ * lax.rsqrt(differ * differ + 0.01)


def kernel(
    dims,
    in_ref, obs_ref, factor_ref, weight_ref, band_ref, back_ref, obs_band_ref,
    main_ref, rest_ref,
    staged, fields, rests, rest_out, halo_out, obs_fields, obs_halo, obs_sm, smooth, result, result_rest,
    edge_out, edge_in,
    f_send, f_recv, fr_send, fr_recv, own_sem, stage_sem,
    h_send, h_recv, oh_send, oh_recv, e_send, e_recv,
    b_send, b_recv, br_send, br_recv, bown_sem, brown_sem,
):
    ens_n, lat_n, local, members, group, rows, width = dims
    half = rows // 2
    pairs = members // 2
    full = width // LANES * LANES
    rest = width - full
    padded = full + LANES
    me = lax.axis_index("ens")
    lat = lax.axis_index("lat")
    has_low = lat > 0
    has_high = lat < lat_n - 1
    variant = (lat == 0).astype(jnp.int32) + 2 * (lat == lat_n - 1).astype(jnp.int32)

    def peer(shift):
        return lax.rem(me + shift, ens_n)

    barrier = pltpu.get_barrier_semaphore()
    for shift in range(1, ens_n):
        pl.semaphore_signal(barrier, inc=1, device_id={"ens": peer(shift)}, device_id_type=MESH)

    @pl.when(has_low)
    def _():
        pl.semaphore_signal(barrier, inc=1, device_id={"lat": lat - 1}, device_id_type=MESH)

    @pl.when(has_high)
    def _():
        pl.semaphore_signal(barrier, inc=1, device_id={"lat": lat + 1}, device_id_type=MESH)

    stage = pltpu.make_async_copy(in_ref, staged, stage_sem)
    stage.start()

    def zero_edges(low):
        at = members if low else members + pairs
        side = 0 if low else 1

        def clear(k, carry):
            def tile(p, inner):
                fields[k, at + p] = jnp.zeros((rows, padded), jnp.float32)
                edge_in[k, side, p] = jnp.zeros((rows, padded), jnp.float32)
                return inner

            lax.fori_loop(0, pairs, tile, 0)
            return carry

        lax.fori_loop(0, group, clear, 0)
        obs_at = group if low else group + group // 2
        for p in range(group // 2):
            obs_fields[obs_at + p] = jnp.zeros((rows, padded), jnp.float32)

    @pl.when(jnp.logical_not(has_low))
    def _():
        zero_edges(True)

    @pl.when(jnp.logical_not(has_high))
    def _():
        zero_edges(False)

    pl.semaphore_wait(barrier, ens_n - 1 + has_low.astype(jnp.int32) + has_high.astype(jnp.int32))

    def f_main(k, shift):
        target = peer(shift)
        return pltpu.make_async_remote_copy(
            src_ref=in_ref.at[:, target * group + k, :, pl.ds(0, full)],
            dst_ref=fields.at[k, pl.ds(me * local, local), :, pl.ds(0, full)],
            send_sem=f_send.at[k, shift], recv_sem=f_recv.at[k, shift],
            device_id={"ens": target}, device_id_type=MESH,
        )

    def f_rest(k, shift):
        target = peer(shift)
        return pltpu.make_async_remote_copy(
            src_ref=rest_out.at[k, target], dst_ref=rests.at[k, me],
            send_sem=fr_send.at[k, shift], recv_sem=fr_recv.at[k, shift],
            device_id={"ens": target}, device_id_type=MESH,
        )

    def f_own(k):
        return pltpu.make_async_copy(
            in_ref.at[:, me * group + k, :, pl.ds(0, full)],
            fields.at[k, pl.ds(me * local, local), :, pl.ds(0, full)],
            own_sem.at[k],
        )

    def start_main(k):
        for shift in range(1, ens_n):
            f_main(k, shift).start()
        f_own(k).start()

    lane = lax.broadcasted_iota(jnp.int32, (rows, LANES), 1)

    def packed(tiles):
        total = tiles[0]
        for m in range(1, local):
            total = jnp.where(lane < m * rest, total, pltpu.roll(tiles[m], m * rest, 1))
        return total

    def start_rest(k):
        for target in range(ens_n):
            tile = packed([
                jnp.concatenate(
                    [staged[m, target * group + k, :, pl.ds(full, rest)],
                     jnp.zeros((rows, LANES - rest), jnp.float32)], axis=1)
                for m in range(local)
            ])
            rest_out[k, target] = tile
        rests[k, me] = rest_out[k, me]
        for shift in range(1, ens_n):
            f_rest(k, shift).start()

    ahead = min(2, group)
    start_main(0)
    stage.wait()
    start_rest(0)
    for k in range(1, ahead):
        start_main(k)
        start_rest(k)

    upper = lax.broadcasted_iota(jnp.int32, (rows, padded), 0) < half

    def turn(tile):
        return pltpu.roll(tile, half, 0)

    def neighbour_copies(source, targets, send, recv):
        return (
            pltpu.make_async_remote_copy(
                src_ref=source[0], dst_ref=targets[1], send_sem=send.at[0], recv_sem=recv.at[1],
                device_id={"lat": lat - 1}, device_id_type=MESH,
            ),
            pltpu.make_async_remote_copy(
                src_ref=source[1], dst_ref=targets[0], send_sem=send.at[1], recv_sem=recv.at[0],
                device_id={"lat": lat + 1}, device_id_type=MESH,
            ),
        )

    def start_both(copies):
        @pl.when(has_low)
        def _():
            copies[0].start()

        @pl.when(has_high)
        def _():
            copies[1].start()

    def recv_both(copies):
        @pl.when(has_low)
        def _():
            copies[1].wait_recv()

        @pl.when(has_high)
        def _():
            copies[0].wait_recv()

    def sent_both(copies):
        @pl.when(has_low)
        def _():
            copies[0].wait_send()

        @pl.when(has_high)
        def _():
            copies[1].wait_send()

    def halo_copies(k):
        return neighbour_copies(
            (halo_out.at[k, 0], halo_out.at[k, 1]),
            (fields.at[k, pl.ds(members, pairs)], fields.at[k, pl.ds(members + pairs, pairs)]),
            h_send.at[k], h_recv.at[k],
        )

    def edge_copies(k):
        return neighbour_copies(
            (edge_out.at[k, 0], edge_out.at[k, 1]), (edge_in.at[k, 0], edge_in.at[k, 1]),
            e_send.at[k], e_recv.at[k],
        )

    couples = group // 2
    obs_copies = neighbour_copies(
        (obs_halo.at[0], obs_halo.at[1]),
        (obs_fields.at[pl.ds(group, couples)], obs_fields.at[pl.ds(group + couples, couples)]),
        oh_send, oh_recv,
    )
    for c in range(group):
        obs_fields[c, :, pl.ds(full, LANES)] = jnp.zeros((rows, LANES), jnp.float32)
        obs_fields[c, :, pl.ds(0, width)] = obs_ref[c]
    for p in range(couples):
        one, two = obs_fields[p], obs_fields[p + couples]
        obs_halo[0, p] = jnp.where(upper, one, turn(two))
        obs_halo[1, p] = jnp.where(upper, turn(one), two)
    start_both(obs_copies)
    recv_both(obs_copies)
    values = obs_fields[...].reshape(2 * group * rows, padded)
    obs_sm[...] = split_dot(obs_band_ref[variant], values).reshape(2 * group, rows, padded)
    lon_blur(obs_sm, group, width)

    def take_fields(k):
        for shift in range(1, ens_n):
            f_main(k, shift).wait_recv()
            f_rest(k, shift).wait_recv()
        f_own(k).wait()

        def unpack(source, carry):
            tile = rests[k, source]
            for m in range(local):
                fields[k, source * local + m, :, pl.ds(full, LANES)] = (
                    pltpu.roll(tile, LANES - m * rest, 1) if m else tile
                )
            return carry

        lax.fori_loop(0, ens_n, unpack, 0)

        def pack_halo(p, carry):
            one, two = fields[k, p], fields[k, p + pairs]
            halo_out[k, 0, p] = jnp.where(upper, one, turn(two))
            halo_out[k, 1, p] = jnp.where(upper, turn(one), two)
            return carry

        lax.fori_loop(0, pairs, pack_halo, 0)
        start_both(halo_copies(k))

        @pl.when(k + ahead < group)
        def _():
            start_main(k + ahead)
            start_rest(k + ahead)

    block = 2 * LANES if padded % (2 * LANES) == 0 else LANES
    total_rows = 2 * members * rows

    def compute(k):
        recv_both(halo_copies(k))

        def smooth_block(b, carry):
            at = pl.ds(pl.multiple_of(b * block, block), block)
            values = fields[k, :, :, at].reshape(total_rows, block)
            smooth[:, :, at] = split_dot(band_ref[variant], values).reshape(2 * members, rows, block)
            return carry

        lax.fori_loop(0, padded // block, smooth_block, 0)
        lon_blur(smooth, members, width)
        weight = factor_ref[me * group + k] * weight_ref[lat]
        pull = 0.95 / (members - 1)
        tiles = padded // LANES

        def couple(i, carry):
            scale, t = i // tiles, i % tiles
            at = pl.ds(pl.multiple_of(t * LANES, LANES), LANES)
            base = scale * members
            held = [smooth[base + m, :, at] for m in range(members)]
            sums = [None] * members
            for m in range(members):
                for other in range(m):
                    force = slope(held[m] - held[other])
                    sums[m] = force if sums[m] is None else sums[m] + force
                    sums[other] = -force if sums[other] is None else sums[other] - force
            analysis = obs_sm[scale * group + k, :, at]
            for m in range(members):
                smooth[base + m, :, at] = weight * (slope(held[m] - analysis) - pull * sums[m])
            return carry

        lax.fori_loop(0, 2 * tiles, couple, 0)
        lon_blur(smooth, members, width)

        def back_block(b, carry):
            at = pl.ds(pl.multiple_of(b * block, block), block)
            values = smooth[:, :, at].reshape(total_rows, block)
            out = split_dot(back_ref[variant], values).reshape(2 * members, rows, block)
            result[k, :, :, at] = out[:members]
            edge_out[k, 0, :, :, at] = out[members : members + pairs]
            edge_out[k, 1, :, :, at] = out[members + pairs :]
            return carry

        lax.fori_loop(0, padded // block, back_block, 0)
        start_both(edge_copies(k))

    def b_main(k, shift):
        target = peer(shift)
        return pltpu.make_async_remote_copy(
            src_ref=result.at[k, pl.ds(target * local, local), :, pl.ds(0, full)],
            dst_ref=main_ref.at[:, me * group + k],
            send_sem=b_send.at[k, shift], recv_sem=b_recv.at[k, shift],
            device_id={"ens": target}, device_id_type=MESH,
        )

    def b_rest(k, shift):
        target = peer(shift)
        return pltpu.make_async_remote_copy(
            src_ref=result_rest.at[k, target], dst_ref=rest_ref.at[me * group + k],
            send_sem=br_send.at[k, shift], recv_sem=br_recv.at[k, shift],
            device_id={"ens": target}, device_id_type=MESH,
        )

    def b_own(k):
        return (
            pltpu.make_async_copy(
                result.at[k, pl.ds(me * local, local), :, pl.ds(0, full)],
                main_ref.at[:, me * group + k], bown_sem.at[k],
            ),
            pltpu.make_async_copy(
                result_rest.at[k, me], rest_ref.at[me * group + k], brown_sem.at[k]
            ),
        )

    def finish(k):
        recv_both(edge_copies(k))

        def add(p, carry):
            low, high = edge_in[k, 0, p], edge_in[k, 1, p]
            result[k, p] = result[k, p] + jnp.where(upper, low, turn(high))
            result[k, p + pairs] = result[k, p + pairs] + jnp.where(upper, turn(low), high)
            return carry

        lax.fori_loop(0, pairs, add, 0)

        def pack(target, carry):
            result_rest[k, target] = packed(
                [result[k, target * local + m, :, pl.ds(full, LANES)] for m in range(local)]
            )
            return carry

        lax.fori_loop(0, ens_n, pack, 0)
        for shift in range(1, ens_n):
            b_main(k, shift).start()
            b_rest(k, shift).start()
        for copy in b_own(k):
            copy.start()

    take_fields(0)

    def turn_of(k, carry):
        @pl.when(k + 1 < group)
        def _():
            take_fields(k + 1)

        compute(k)

        @pl.when(k > 0)
        def _():
            finish(k - 1)

        return carry

    lax.fori_loop(0, group, turn_of, 0)
    finish(group - 1)

    sent_both(obs_copies)

    def drain(k, carry):
        for shift in range(1, ens_n):
            f_main(k, shift).wait_send()
            f_rest(k, shift).wait_send()
            b_main(k, shift).wait()
            b_rest(k, shift).wait()
        for copy in b_own(k):
            copy.wait()
        sent_both(halo_copies(k))
        sent_both(edge_copies(k))
        return carry

    lax.fori_loop(0, group, drain, 0)


def unpack_kernel(rest, main_ref, rest_ref, out_ref):
    local, _, _, full = main_ref.shape
    tile = rest_ref[...]
    for m in range(local):
        out_ref[m, :, :, pl.ds(0, full)] = main_ref[m]
        out_ref[m, :, :, pl.ds(full, rest)] = tile[:, :, m * rest : (m + 1) * rest]


def body(prediction_array, verifying_analysis, variable_penalty_factor):
    local, channels, rows, width = prediction_array.shape
    group = verifying_analysis.shape[0]
    ens_n, lat_n = lax.axis_size("ens"), lax.axis_size("lat")
    members = local * ens_n
    pairs = members // 2
    full = width // LANES * LANES
    rest = width - full
    padded = full + LANES
    assert rows % 8 == 0 and rows // 2 >= COARSE and local * rest <= LANES and channels == group * ens_n
    assert members % 2 == 0 and group % 2 == 0 and LANES - rest >= 4 * COARSE

    bands = band_matrices(members, rows)
    band = jnp.asarray(bands, jnp.bfloat16)
    back = jnp.asarray(np.ascontiguousarray(bands.transpose(0, 2, 1)), jnp.bfloat16)
    obs_band = jnp.asarray(band_matrices(group, rows), jnp.bfloat16)
    ids = np.arange(lat_n * rows).astype(np.float32)
    degrees = np.float32(0.25) * (ids - np.float32((lat_n * rows - 1) / 2.0))
    weights = np.cos(degrees * np.float32(np.pi / 180.0)).astype(np.float32).reshape(lat_n, rows, 1)
    weights = jnp.asarray(np.broadcast_to(weights, (lat_n, rows, LANES)))

    dims = (ens_n, lat_n, local, members, group, rows, width)
    vmem = pl.BlockSpec(memory_space=pltpu.VMEM)
    hbm = pl.BlockSpec(memory_space=pl.ANY)
    f32 = jnp.float32
    dma = pltpu.SemaphoreType.DMA
    cells = group * padded * rows
    main, rests = pl.pallas_call(
        functools.partial(kernel, dims),
        out_shape=(
            jax.ShapeDtypeStruct((local, channels, rows, full), f32),
            jax.ShapeDtypeStruct((channels, rows, LANES), f32),
        ),
        in_specs=[hbm, vmem, pl.BlockSpec(memory_space=pltpu.SMEM), vmem, vmem, vmem, vmem],
        out_specs=(hbm, hbm),
        scratch_shapes=[
            pltpu.VMEM((local, channels, rows, width), f32),
            pltpu.VMEM((group, members + 2 * pairs, rows, padded), f32),
            pltpu.VMEM((group, ens_n, rows, LANES), f32),
            pltpu.VMEM((group, ens_n, rows, LANES), f32),
            pltpu.VMEM((group, 2, pairs, rows, padded), f32),
            pltpu.VMEM((2 * group, rows, padded), f32),
            pltpu.VMEM((2, group // 2, rows, padded), f32),
            pltpu.VMEM((2 * group, rows, padded), f32),
            pltpu.VMEM((2 * members, rows, padded), f32),
            pltpu.VMEM((group, members, rows, padded), f32),
            pltpu.VMEM((group, ens_n, rows, LANES), f32),
            pltpu.VMEM((group, 2, pairs, rows, padded), f32),
            pltpu.VMEM((group, 2, pairs, rows, padded), f32),
            dma((group, ens_n)), dma((group, ens_n)), dma((group, ens_n)), dma((group, ens_n)),
            dma((group,)), dma,
            dma((group, 2)), dma((group, 2)), dma((2,)), dma((2,)), dma((group, 2)), dma((group, 2)),
            dma((group, ens_n)), dma((group, ens_n)), dma((group, ens_n)), dma((group, ens_n)),
            dma((group,)), dma((group,)),
        ],
        compiler_params=pltpu.CompilerParams(
            collective_id=0, has_side_effects=True, vmem_limit_bytes=48 * 1024 * 1024
        ),
        cost_estimate=pl.CostEstimate(
            flops=cells * members * members * 6, bytes_accessed=cells * members * 8,
            transcendentals=cells * members * members,
        ),
    )(prediction_array, verifying_analysis, variable_penalty_factor, weights, band, back, obs_band)

    part = group
    return pl.pallas_call(
        functools.partial(unpack_kernel, rest),
        grid=(channels // part,),
        out_shape=jax.ShapeDtypeStruct((local, channels, rows, width), f32),
        in_specs=[
            pl.BlockSpec((local, part, rows, full), lambda i: (0, i, 0, 0)),
            pl.BlockSpec((part, rows, LANES), lambda i: (i, 0, 0)),
        ],
        out_specs=pl.BlockSpec((local, part, rows, width), lambda i: (0, i, 0, 0)),
    )(main, rests)


def solution(mesh):
    placed = (P("ens", None, "lat", None), P("ens", "lat", None), P())
    return jax.shard_map(
        body, mesh=mesh, in_specs=placed, out_specs=P("ens", None, "lat", None), check_vma=False
    )
```

time: 301 us -> 125 us (0.42)
  Pallas kernels: 0 us -> 117 us
  other arithmetic: 91.8 us -> 0 us
  blocking collectives: 76.9 us -> 0 us
  local copies, waits for them, and re-layouts: 64.7 us -> 7.45 us
  waiting for transfers between devices: 34.8 us -> 0 us
  starting transfers between devices: 29.9 us -> 0 us
    pallas_call x0 -> x2, Pallas kernels: none -> 117 us  [the longest x1 113 us: body(): pl.pallas_call(functools.partial(kernel, dims), out_shape=(jax.ShapeDtype...]
    all_to_all x2 -> x0, blocking collectives: 76.9 us -> none  [the longest x1 38.5 us: body(): lax.all_to_all(combined.reshape(all_members, group_size, parallel_number,...]
    reduce_sum x32 -> x0, other arithmetic: 50.6 us -> none  [single(): return jnp.sum(slope(member[None] - smooth_fc), axis=0)]
    ppermute x12 -> x0, waiting for transfers between devices: 34.8 us -> none  [the longest x6 22 us: with_halo(): lax.ppermute(lax.slice_in_dim(block, 0, width, axis=dim), axis, backward)]
    ppermute x12 -> x0, starting transfers between devices: 29.9 us -> none  [the longest x6 15.8 us: with_halo(): lax.ppermute(lax.slice_in_dim(block, block.shape[dim] - width, None, axis...]
    dynamic_update_slice x32 -> x0, local copies, waits for them, and re-layouts: 22.3 us -> none  [couple_derivative(): pulls = lax.map(single, smooth_fc)]
    add x7 -> x0, other arithmetic: 20.5 us -> none  [the longest x6 17.5 us: normal_kernel_smoother(): 0.25 * extended[:, :-2] + 0.5 * extended[:, 1:-1] + 0.25 * extended[:, 2:]]
    sub x32 -> x0, local copies, waits for them, and re-layouts: 15.4 us -> none  [single(): return jnp.sum(slope(member[None] - smooth_fc), axis=0)]
  transfers between devices with their start and end apart: 12 -> 0, of which waited for: 10 -> 0; matrix products, arithmetic and copies ran while one was open for 8% -> 0% of each run, Pallas kernels for 0% -> 0%
where the time goes in v1:
time: 125 us; the launch traced here: 124 us
  Pallas kernels  117 us (94%)
  local copies, waits for them, and re-layouts  7.45 us (6%)
    pallas_call x1, Pallas kernels, body(): pl.pallas_call(functools.partial(kernel, dims), out_shape=(jax.ShapeDtype...  113 us
    unnamed x14, local copies, waits for them, and re-layouts  6.7 us
    pallas_call x1, Pallas kernels, body(): pl.pallas_call(functools.partial(unpack_kernel, rest), grid=(channels //...  4.29 us

profile of v1, /device:TPU:11, one launch (start us, length us, event | category | flops | bytes accessed | tf_op | source)
XLA Modules:
  0.0 124.4 jit_solution(6169811261225621334)
XLA Ops:
  0.0 0.8 jit_solution_.3.weight_ref
  0.8 0.0 copy-start.2
  0.8 0.9 copy-done.2
  1.7 0.0 copy-start.3
  1.7 0.7 copy-done.3
  2.3 0.0 copy-start.4
  2.3 1.0 copy-done.4
  3.4 0.0 copy-start.5
  3.4 1.0 copy-done.5
  4.4 0.0 copy-start.6
  4.4 0.8 copy-done.6
  5.3 112.6 %shard_map.73 = (f32[4,16,8,1408]{3,2,1,0:T(8,128)S(1)}, f32[16,8,128]{2,1,0:T(8,128)S(1)}) custom-call(f32[4,16,8,1440]{3,2,1,0:T(8,128)} %in_ref.1, f32[4,8,1440]{2,1,0:T(8,128)S(1)} %copy-done.2, f32[16]{0:T(128)S(1)} %copy-done.3, f32[8,8,128]{2,1,0:T(8,128)S(1)} %jit_solution_.3.weight_ref, bf16[4,256,256]{2,1,0:T(8,128)(2,1)S(1)} %copy-done.5, ...), custom_call_target="tpu_custom_call" | custom-call | flops 75497472 | bytes 6291456 | tf_op jit(solution)/shard_map/pallas_call | solution.py:493
  117.9 0.0 copy-start
  117.9 1.6 %copy-done = f32[4,16,8,1408]{3,2,1,0:T(8,128)} copy-done((f32[4,16,8,1408]{3,2,1,0:T(8,128)}, f32[4,16,8,1408]{3,2,1,0:T(8,128)S(1)}, u32[]{:S(2)}) %copy-start) | copy-done | bytes 2883608
  119.4 0.0 copy-start.1
  119.4 0.6 copy-done.1
  120.1 4.3 %shard_map.74 = f32[4,16,8,1440]{3,2,1,0:T(8,128)} custom-call(f32[4,16,8,1408]{3,2,1,0:T(8,128)} %copy-done, f32[16,8,128]{2,1,0:T(8,128)} %copy-done.1), custom_call_target="tpu_custom_call" | custom-call | tf_op jit(solution)/shard_map/pallas_call | solution.py:531
Async XLA Ops:
  0.8 0.9 copy-start.2
  1.7 0.7 copy-start.3
  2.3 1.0 copy-start.4
  3.4 1.0 copy-start.5
  4.4 0.8 copy-start.6
  117.9 1.6 %copy-start = (f32[4,16,8,1408]{3,2,1,0:T(8,128)}, f32[4,16,8,1408]{3,2,1,0:T(8,128)S(1)}, u32[]{:S(2)}) copy-start(f32[4,16,8,1408]{3,2,1,0:T(8,128)S(1)} %get-tuple-element.7.main_ref) | copy-start | bytes 8650756
  119.4 0.6 copy-start.1

commit v2 on v1

--- a/solution.py
+++ b/solution.py
@@ -1,4 +1,5 @@
 import functools
+import math
 
 import jax
 import jax.numpy as jnp
@@ -45,14 +46,13 @@
     return out
 
 
-def split_dot(matrix, values):
-    first = values.astype(jnp.bfloat16)
-    rest = values - first.astype(jnp.float32)
-    second = rest.astype(jnp.bfloat16)
-    third = (rest - second.astype(jnp.float32)).astype(jnp.bfloat16)
-    total = jnp.dot(matrix, third, preferred_element_type=jnp.float32)
-    total = total + jnp.dot(matrix, second, preferred_element_type=jnp.float32)
-    return total + jnp.dot(matrix, first, preferred_element_type=jnp.float32)
+def split_dot(matrix, values, parts):
+    pieces = []
+    for _ in range(parts):
+        piece = values.astype(jnp.bfloat16)
+        pieces.append(piece)
+        values = values - piece.astype(jnp.float32)
+    return jnp.dot(matrix, jnp.concatenate(pieces, axis=0), preferred_element_type=jnp.float32)
 
 
 def wrapped(tiles, width):
@@ -66,21 +66,22 @@
     return jnp.concatenate([tiles[:, : whole * LANES], last], axis=1)
 
 
-def lon_pass(tiles):
+def lon_pass(tiles, passes):
     size = tiles.shape[1]
-    return 0.25 * (pltpu.roll(tiles, 1, 1) + pltpu.roll(tiles, size - 1, 1)) + 0.5 * tiles
+    total = math.comb(2 * passes, passes) / 4.0**passes * tiles
+    for far in range(1, passes + 1):
+        both = pltpu.roll(tiles, far, 1) + pltpu.roll(tiles, size - far, 1)
+        total = total + math.comb(2 * passes, passes + far) / 4.0**passes * both
+    return total
 
 
 def lon_blur(ref, count, width):
     def step(field, carry):
-        ref[field] = lon_pass(wrapped(ref[field], width))
-        coarse = wrapped(ref[count + field], width)
-        for _ in range(COARSE):
-            coarse = lon_pass(coarse)
-        ref[count + field] = coarse
+        ref[field] = lon_pass(wrapped(ref[field], width), 1)
+        ref[count + field] = lon_pass(wrapped(ref[count + field], width), COARSE)
         return carry
 
-    lax.fori_loop(0, count, step, 0)
+    lax.fori_loop(0, count, step, 0, unroll=2)
 
 
 def slope(differ):
@@ -89,13 +90,14 @@
 
 def kernel(
     dims,
-    in_ref, obs_ref, factor_ref, weight_ref, band_ref, back_ref, obs_band_ref,
-    main_ref, rest_ref,
+    in_ref, obs_hbm, factor_ref, weight_hbm, band_hbm, back_hbm, obs_band_hbm,
+    out_ref,
+    main_ref, rest_ref, obs_ref, weight_ref, band_ref, back_ref, obs_band_ref,
     staged, fields, rests, rest_out, halo_out, obs_fields, obs_halo, obs_sm, smooth, result, result_rest,
     edge_out, edge_in,
     f_send, f_recv, fr_send, fr_recv, own_sem, stage_sem,
     h_send, h_recv, oh_send, oh_recv, e_send, e_recv,
-    b_send, b_recv, br_send, br_recv, bown_sem, brown_sem,
+    b_send, b_recv, br_send, br_recv, bown_sem, load_sem, out_sem,
 ):
     ens_n, lat_n, local, members, group, rows, width = dims
     half = rows // 2
@@ -126,6 +128,18 @@
 
     stage = pltpu.make_async_copy(in_ref, staged, stage_sem)
     stage.start()
+    loads = [
+        pltpu.make_async_copy(source, target, load_sem.at[i])
+        for i, (source, target) in enumerate((
+            (obs_hbm, obs_ref),
+            (weight_hbm.at[lat], weight_ref),
+            (band_hbm.at[variant], band_ref),
+            (back_hbm.at[variant], back_ref),
+            (obs_band_hbm.at[variant], obs_band_ref),
+        ))
+    ]
+    for load in loads:
+        load.start()
 
     def zero_edges(low):
         at = members if low else members + pairs
@@ -209,10 +223,6 @@
     start_main(0)
     stage.wait()
     start_rest(0)
-    for k in range(1, ahead):
-        start_main(k)
-        start_rest(k)
-
     upper = lax.broadcasted_iota(jnp.int32, (rows, padded), 0) < half
 
     def turn(tile):
@@ -270,6 +280,8 @@
             e_send.at[k], e_recv.at[k],
         )
 
+    for load in loads:
+        load.wait()
     couples = group // 2
     obs_copies = neighbour_copies(
         (obs_halo.at[0], obs_halo.at[1]),
@@ -284,9 +296,12 @@
         obs_halo[0, p] = jnp.where(upper, one, turn(two))
         obs_halo[1, p] = jnp.where(upper, turn(one), two)
     start_both(obs_copies)
+    for k in range(1, ahead):
+        start_main(k)
+        start_rest(k)
     recv_both(obs_copies)
     values = obs_fields[...].reshape(2 * group * rows, padded)
-    obs_sm[...] = split_dot(obs_band_ref[variant], values).reshape(2 * group, rows, padded)
+    obs_sm[...] = split_dot(obs_band_ref[...], values, 3).reshape(2 * group, rows, padded)
     lon_blur(obs_sm, group, width)
 
     def take_fields(k):
@@ -322,18 +337,18 @@
     block = 2 * LANES if padded % (2 * LANES) == 0 else LANES
     total_rows = 2 * members * rows
 
-    def compute(k):
+    def forward(k):
         recv_both(halo_copies(k))
 
         def smooth_block(b, carry):
             at = pl.ds(pl.multiple_of(b * block, block), block)
             values = fields[k, :, :, at].reshape(total_rows, block)
-            smooth[:, :, at] = split_dot(band_ref[variant], values).reshape(2 * members, rows, block)
-            return carry
-
-        lax.fori_loop(0, padded // block, smooth_block, 0)
+            smooth[:, :, at] = split_dot(band_ref[...], values, 3).reshape(2 * members, rows, block)
+            return carry
+
+        lax.fori_loop(0, padded // block, smooth_block, 0, unroll=3 if padded // block % 3 == 0 else 1)
         lon_blur(smooth, members, width)
-        weight = factor_ref[me * group + k] * weight_ref[lat]
+        weight = factor_ref[me * group + k] * weight_ref[...]
         pull = 0.95 / (members - 1)
         tiles = padded // LANES
 
@@ -354,25 +369,27 @@
             return carry
 
         lax.fori_loop(0, 2 * tiles, couple, 0)
+
+    def backward(k):
         lon_blur(smooth, members, width)
 
         def back_block(b, carry):
             at = pl.ds(pl.multiple_of(b * block, block), block)
             values = smooth[:, :, at].reshape(total_rows, block)
-            out = split_dot(back_ref[variant], values).reshape(2 * members, rows, block)
+            out = split_dot(back_ref[...], values, 2).reshape(2 * members, rows, block)
             result[k, :, :, at] = out[:members]
             edge_out[k, 0, :, :, at] = out[members : members + pairs]
             edge_out[k, 1, :, :, at] = out[members + pairs :]
             return carry
 
-        lax.fori_loop(0, padded // block, back_block, 0)
+        lax.fori_loop(0, padded // block, back_block, 0, unroll=3 if padded // block % 3 == 0 else 1)
         start_both(edge_copies(k))
 
     def b_main(k, shift):
         target = peer(shift)
         return pltpu.make_async_remote_copy(
             src_ref=result.at[k, pl.ds(target * local, local), :, pl.ds(0, full)],
-            dst_ref=main_ref.at[:, me * group + k],
+            dst_ref=main_ref.at[:, me * group + k, :, pl.ds(0, full)],
             send_sem=b_send.at[k, shift], recv_sem=b_recv.at[k, shift],
             device_id={"ens": target}, device_id_type=MESH,
         )
@@ -386,14 +403,15 @@
         )
 
     def b_own(k):
-        return (
-            pltpu.make_async_copy(
-                result.at[k, pl.ds(me * local, local), :, pl.ds(0, full)],
-                main_ref.at[:, me * group + k], bown_sem.at[k],
-            ),
-            pltpu.make_async_copy(
-                result_rest.at[k, me], rest_ref.at[me * group + k], brown_sem.at[k]
-            ),
+        return pltpu.make_async_copy(
+            result.at[k, pl.ds(me * local, local), :, pl.ds(0, full)],
+            main_ref.at[:, me * group + k, :, pl.ds(0, full)], bown_sem.at[k],
+        )
+
+    def write(k, source):
+        channel = source * group + k
+        return pltpu.make_async_copy(
+            main_ref.at[:, channel], out_ref.at[:, channel], out_sem.at[k, source]
         )
 
     def finish(k):
@@ -417,17 +435,19 @@
         for shift in range(1, ens_n):
             b_main(k, shift).start()
             b_rest(k, shift).start()
-        for copy in b_own(k):
-            copy.start()
+        b_own(k).start()
+        rest_ref[me * group + k] = result_rest[k, me]
 
     take_fields(0)
 
     def turn_of(k, carry):
+        forward(k)
+
         @pl.when(k + 1 < group)
         def _():
             take_fields(k + 1)
 
-        compute(k)
+        backward(k)
 
         @pl.when(k > 0)
         def _():
@@ -441,26 +461,37 @@
     sent_both(obs_copies)
 
     def drain(k, carry):
+        for shift in range(1, ens_n):
+            b_main(k, shift).wait_recv()
+            b_rest(k, shift).wait_recv()
+        b_own(k).wait()
+
+        def unpack(source, inner):
+            channel = source * group + k
+            tile = rest_ref[channel]
+            for m in range(local):
+                main_ref[m, channel, :, pl.ds(full, rest)] = tile[:, m * rest : (m + 1) * rest]
+            write(k, source).start()
+            return inner
+
+        lax.fori_loop(0, ens_n, unpack, 0)
         for shift in range(1, ens_n):
             f_main(k, shift).wait_send()
             f_rest(k, shift).wait_send()
-            b_main(k, shift).wait()
-            b_rest(k, shift).wait()
-        for copy in b_own(k):
-            copy.wait()
+            b_main(k, shift).wait_send()
+            b_rest(k, shift).wait_send()
         sent_both(halo_copies(k))
         sent_both(edge_copies(k))
         return carry
 
     lax.fori_loop(0, group, drain, 0)
 
-
-def unpack_kernel(rest, main_ref, rest_ref, out_ref):
-    local, _, _, full = main_ref.shape
-    tile = rest_ref[...]
-    for m in range(local):
-        out_ref[m, :, :, pl.ds(0, full)] = main_ref[m]
-        out_ref[m, :, :, pl.ds(full, rest)] = tile[:, :, m * rest : (m + 1) * rest]
+    def close(k, carry):
+        for source in range(ens_n):
+            write(k, source).wait()
+        return carry
+
+    lax.fori_loop(0, group, close, 0)
 
 
 def body(prediction_array, verifying_analysis, variable_penalty_factor):
@@ -476,29 +507,33 @@
     assert members % 2 == 0 and group % 2 == 0 and LANES - rest >= 4 * COARSE
 
     bands = band_matrices(members, rows)
-    band = jnp.asarray(bands, jnp.bfloat16)
-    back = jnp.asarray(np.ascontiguousarray(bands.transpose(0, 2, 1)), jnp.bfloat16)
-    obs_band = jnp.asarray(band_matrices(group, rows), jnp.bfloat16)
+    band = jnp.asarray(np.concatenate([bands] * 3, axis=2), jnp.bfloat16)
+    back = jnp.asarray(np.concatenate([bands.transpose(0, 2, 1)] * 2, axis=2), jnp.bfloat16)
+    obs_bands = band_matrices(group, rows)
+    obs_band = jnp.asarray(np.concatenate([obs_bands] * 3, axis=2), jnp.bfloat16)
     ids = np.arange(lat_n * rows).astype(np.float32)
     degrees = np.float32(0.25) * (ids - np.float32((lat_n * rows - 1) / 2.0))
     weights = np.cos(degrees * np.float32(np.pi / 180.0)).astype(np.float32).reshape(lat_n, rows, 1)
     weights = jnp.asarray(np.broadcast_to(weights, (lat_n, rows, LANES)))
 
     dims = (ens_n, lat_n, local, members, group, rows, width)
-    vmem = pl.BlockSpec(memory_space=pltpu.VMEM)
     hbm = pl.BlockSpec(memory_space=pl.ANY)
     f32 = jnp.float32
     dma = pltpu.SemaphoreType.DMA
     cells = group * padded * rows
-    main, rests = pl.pallas_call(
+    return pl.pallas_call(
         functools.partial(kernel, dims),
-        out_shape=(
-            jax.ShapeDtypeStruct((local, channels, rows, full), f32),
-            jax.ShapeDtypeStruct((channels, rows, LANES), f32),
-        ),
-        in_specs=[hbm, vmem, pl.BlockSpec(memory_space=pltpu.SMEM), vmem, vmem, vmem, vmem],
-        out_specs=(hbm, hbm),
+        out_shape=jax.ShapeDtypeStruct((local, channels, rows, width), f32),
+        in_specs=[hbm, hbm, pl.BlockSpec(memory_space=pltpu.SMEM), hbm, hbm, hbm, hbm],
+        out_specs=hbm,
         scratch_shapes=[
+            pltpu.VMEM((local, channels, rows, width), f32),
+            pltpu.VMEM((channels, rows, LANES), f32),
+            pltpu.VMEM(verifying_analysis.shape, f32),
+            pltpu.VMEM(weights.shape[1:], f32),
+            pltpu.VMEM(band.shape[1:], jnp.bfloat16),
+            pltpu.VMEM(back.shape[1:], jnp.bfloat16),
+            pltpu.VMEM(obs_band.shape[1:], jnp.bfloat16),
             pltpu.VMEM((local, channels, rows, width), f32),
             pltpu.VMEM((group, members + 2 * pairs, rows, padded), f32),
             pltpu.VMEM((group, ens_n, rows, LANES), f32),
@@ -516,7 +551,7 @@
             dma((group,)), dma,
             dma((group, 2)), dma((group, 2)), dma((2,)), dma((2,)), dma((group, 2)), dma((group, 2)),
             dma((group, ens_n)), dma((group, ens_n)), dma((group, ens_n)), dma((group, ens_n)),
-            dma((group,)), dma((group,)),
+            dma((group,)), dma((5,)), dma((group, ens_n)),
         ],
         compiler_params=pltpu.CompilerParams(
             collective_id=0, has_side_effects=True, vmem_limit_bytes=48 * 1024 * 1024
@@ -527,18 +562,6 @@
         ),
     )(prediction_array, verifying_analysis, variable_penalty_factor, weights, band, back, obs_band)
 
-    part = group
-    return pl.pallas_call(
-        functools.partial(unpack_kernel, rest),
-        grid=(channels // part,),
-        out_shape=jax.ShapeDtypeStruct((local, channels, rows, width), f32),
-        in_specs=[
-            pl.BlockSpec((local, part, rows, full), lambda i: (0, i, 0, 0)),
-            pl.BlockSpec((part, rows, LANES), lambda i: (i, 0, 0)),
-        ],
-        out_specs=pl.BlockSpec((local, part, rows, width), lambda i: (0, i, 0, 0)),
-    )(main, rests)
-
 
 def solution(mesh):
     placed = (P("ens", None, "lat", None), P("ens", "lat", None), P())

time: 125 us -> 108 us (0.86)
  Pallas kernels: 117 us -> 99.8 us
    pallas_call x2 -> x1, Pallas kernels: 117 us -> 99.8 us  [body(): pl.pallas_call(functools.partial(kernel, dims), out_shape=jax.ShapeDtypeS...]
    unnamed x14 -> x11, local copies, waits for them, and re-layouts: 6.7 us -> 6.79 us
where the time goes in v2:
time: 108 us; the launch traced here: 107 us
  Pallas kernels  99.8 us (92%)
  local copies, waits for them, and re-layouts  7.54 us (7%)
    pallas_call x1, Pallas kernels, body(): pl.pallas_call(functools.partial(kernel, dims), out_shape=jax.ShapeDtypeS...  99.8 us
    unnamed x11, local copies, waits for them, and re-layouts  6.79 us

profile of v2, /device:TPU:11, one launch (start us, length us, event | category | flops | bytes accessed | tf_op | source)
XLA Modules:
  0.0 107.4 jit_solution(6651444849455859344)
XLA Ops:
  0.0 0.8 jit_solution_.3.weight_hbm
  0.8 0.0 copy-start
  0.8 0.9 copy-done
  1.7 0.0 copy-start.1
  1.7 0.7 copy-done.1
  2.3 0.0 copy-start.2
  2.3 1.4 %copy-done.2 = bf16[4,256,768]{2,1,0:T(8,128)(2,1)S(1)} copy-done((bf16[4,256,768]{2,1,0:T(8,128)(2,1)S(1)}, bf16[4,256,768]{2,1,0:T(8,128)(2,1)}, u32[]{:S(2)}) %copy-start.2) | copy-done | bytes 1572888
  3.8 0.0 copy-start.3
  3.8 1.2 %copy-done.3 = bf16[4,256,512]{2,1,0:T(8,128)(2,1)S(1)} copy-done((bf16[4,256,512]{2,1,0:T(8,128)(2,1)S(1)}, bf16[4,256,512]{2,1,0:T(8,128)(2,1)}, u32[]{:S(2)}) %copy-start.3) | copy-done | bytes 1048600
  5.0 0.0 copy-start.4
  5.0 0.9 copy-done.4
  5.9 99.8 %shard_map.73 = f32[4,16,8,1440]{3,2,1,0:T(8,128)S(1)} custom-call(f32[4,16,8,1440]{3,2,1,0:T(8,128)} %in_ref.1, f32[4,8,1440]{2,1,0:T(8,128)S(1)} %copy-done, f32[16]{0:T(128)S(1)} %copy-done.1, f32[8,8,128]{2,1,0:T(8,128)S(1)} %jit_solution_.3.weight_hbm, bf16[4,256,768]{2,1,0:T(8,128)(2,1)S(1)} %copy-done.2, bf16[4,256,512]{2,1,0:T(8,128)(2,1)S(1)} %copy-done.3, ...), custom_call_target="tpu_custom_call" | custom-call | flops 75497472 | bytes 6291456 | tf_op jit(solution)/shard_map/pallas_call | solution.py:524
  105.7 1.7 %copy.9 = f32[4,16,8,1440]{3,2,1,0:T(8,128)} copy(f32[4,16,8,1440]{3,2,1,0:T(8,128)S(1)} %shard_map.73) | data formatting | bytes 5898240
Async XLA Ops:
  0.8 0.9 copy-start
  1.7 0.7 copy-start.1
  2.3 1.4 %copy-start.2 = (bf16[4,256,768]{2,1,0:T(8,128)(2,1)S(1)}, bf16[4,256,768]{2,1,0:T(8,128)(2,1)}, u32[]{:S(2)}) copy-start(bf16[4,256,768]{2,1,0:T(8,128)(2,1)} %constant.8.clone.band_hbm) | copy-start | bytes 4718596
  3.8 1.2 %copy-start.3 = (bf16[4,256,512]{2,1,0:T(8,128)(2,1)S(1)}, bf16[4,256,512]{2,1,0:T(8,128)(2,1)}, u32[]{:S(2)}) copy-start(bf16[4,256,512]{2,1,0:T(8,128)(2,1)} %constant.9.clone.back_hbm) | copy-start | bytes 3145732
  5.0 0.9 copy-start.4

commit v3 on v2

--- a/solution.py
+++ b/solution.py
@@ -81,7 +81,7 @@
         ref[count + field] = lon_pass(wrapped(ref[count + field], width), COARSE)
         return carry
 
-    lax.fori_loop(0, count, step, 0, unroll=2)
+    lax.fori_loop(0, count, step, 0, unroll=4 if count % 4 == 0 else 2)
 
 
 def slope(differ):
@@ -105,6 +105,7 @@
     full = width // LANES * LANES
     rest = width - full
     padded = full + LANES
+    total_rows = 2 * members * rows
     me = lax.axis_index("ens")
     lat = lax.axis_index("lat")
     has_low = lat > 0
@@ -133,8 +134,8 @@
         for i, (source, target) in enumerate((
             (obs_hbm, obs_ref),
             (weight_hbm.at[lat], weight_ref),
-            (band_hbm.at[variant], band_ref),
-            (back_hbm.at[variant], back_ref),
+            *((band_hbm.at[variant], band_ref.at[:, pl.ds(part * total_rows, total_rows)]) for part in range(3)),
+            *((back_hbm.at[variant], back_ref.at[:, pl.ds(part * total_rows, total_rows)]) for part in range(2)),
             (obs_band_hbm.at[variant], obs_band_ref),
         ))
     ]
@@ -296,13 +297,13 @@
         obs_halo[0, p] = jnp.where(upper, one, turn(two))
         obs_halo[1, p] = jnp.where(upper, turn(one), two)
     start_both(obs_copies)
-    for k in range(1, ahead):
-        start_main(k)
-        start_rest(k)
     recv_both(obs_copies)
     values = obs_fields[...].reshape(2 * group * rows, padded)
     obs_sm[...] = split_dot(obs_band_ref[...], values, 3).reshape(2 * group, rows, padded)
     lon_blur(obs_sm, group, width)
+    for k in range(1, ahead):
+        start_main(k)
+        start_rest(k)
 
     def take_fields(k):
         for shift in range(1, ens_n):
@@ -318,7 +319,7 @@
                 )
             return carry
 
-        lax.fori_loop(0, ens_n, unpack, 0)
+        lax.fori_loop(0, ens_n, unpack, 0, unroll=True)
 
         def pack_halo(p, carry):
             one, two = fields[k, p], fields[k, p + pairs]
@@ -326,7 +327,7 @@
             halo_out[k, 1, p] = jnp.where(upper, turn(one), two)
             return carry
 
-        lax.fori_loop(0, pairs, pack_halo, 0)
+        lax.fori_loop(0, pairs, pack_halo, 0, unroll=4 if pairs % 4 == 0 else 1)
         start_both(halo_copies(k))
 
         @pl.when(k + ahead < group)
@@ -335,7 +336,6 @@
             start_rest(k + ahead)
 
     block = 2 * LANES if padded % (2 * LANES) == 0 else LANES
-    total_rows = 2 * members * rows
 
     def forward(k):
         recv_both(halo_copies(k))
@@ -348,7 +348,7 @@
 
         lax.fori_loop(0, padded // block, smooth_block, 0, unroll=3 if padded // block % 3 == 0 else 1)
         lon_blur(smooth, members, width)
-        weight = factor_ref[me * group + k] * weight_ref[...]
+        weight = factor_ref[me * group + k] * jnp.broadcast_to(weight_ref[:, :1], (rows, LANES))
         pull = 0.95 / (members - 1)
         tiles = padded // LANES
 
@@ -423,7 +423,7 @@
             result[k, p + pairs] = result[k, p + pairs] + jnp.where(upper, turn(low), high)
             return carry
 
-        lax.fori_loop(0, pairs, add, 0)
+        lax.fori_loop(0, pairs, add, 0, unroll=4 if pairs % 4 == 0 else 1)
 
         def pack(target, carry):
             result_rest[k, target] = packed(
@@ -431,7 +431,7 @@
             )
             return carry
 
-        lax.fori_loop(0, ens_n, pack, 0)
+        lax.fori_loop(0, ens_n, pack, 0, unroll=True)
         for shift in range(1, ens_n):
             b_main(k, shift).start()
             b_rest(k, shift).start()
@@ -443,15 +443,15 @@
     def turn_of(k, carry):
         forward(k)
 
+        @pl.when(k > 0)
+        def _():
+            finish(k - 1)
+
         @pl.when(k + 1 < group)
         def _():
             take_fields(k + 1)
 
         backward(k)
-
-        @pl.when(k > 0)
-        def _():
-            finish(k - 1)
 
         return carry
 
@@ -507,14 +507,15 @@
     assert members % 2 == 0 and group % 2 == 0 and LANES - rest >= 4 * COARSE
 
     bands = band_matrices(members, rows)
-    band = jnp.asarray(np.concatenate([bands] * 3, axis=2), jnp.bfloat16)
-    back = jnp.asarray(np.concatenate([bands.transpose(0, 2, 1)] * 2, axis=2), jnp.bfloat16)
+    band = jnp.asarray(bands, jnp.bfloat16)
+    back = jnp.asarray(bands.transpose(0, 2, 1), jnp.bfloat16)
+    square = bands.shape[1]
     obs_bands = band_matrices(group, rows)
     obs_band = jnp.asarray(np.concatenate([obs_bands] * 3, axis=2), jnp.bfloat16)
     ids = np.arange(lat_n * rows).astype(np.float32)
     degrees = np.float32(0.25) * (ids - np.float32((lat_n * rows - 1) / 2.0))
     weights = np.cos(degrees * np.float32(np.pi / 180.0)).astype(np.float32).reshape(lat_n, rows, 1)
-    weights = jnp.asarray(np.broadcast_to(weights, (lat_n, rows, LANES)))
+    weights = jnp.asarray(np.pad(weights, ((0, 0), (0, 0), (0, LANES - 1))))
 
     dims = (ens_n, lat_n, local, members, group, rows, width)
     hbm = pl.BlockSpec(memory_space=pl.ANY)
@@ -531,8 +532,8 @@
             pltpu.VMEM((channels, rows, LANES), f32),
             pltpu.VMEM(verifying_analysis.shape, f32),
             pltpu.VMEM(weights.shape[1:], f32),
-            pltpu.VMEM(band.shape[1:], jnp.bfloat16),
-            pltpu.VMEM(back.shape[1:], jnp.bfloat16),
+            pltpu.VMEM((square, 3 * square), jnp.bfloat16),
+            pltpu.VMEM((square, 2 * square), jnp.bfloat16),
             pltpu.VMEM(obs_band.shape[1:], jnp.bfloat16),
             pltpu.VMEM((local, channels, rows, width), f32),
             pltpu.VMEM((group, members + 2 * pairs, rows, padded), f32),
@@ -551,10 +552,10 @@
             dma((group,)), dma,
             dma((group, 2)), dma((group, 2)), dma((2,)), dma((2,)), dma((group, 2)), dma((group, 2)),
             dma((group, ens_n)), dma((group, ens_n)), dma((group, ens_n)), dma((group, ens_n)),
-            dma((group,)), dma((5,)), dma((group, ens_n)),
+            dma((group,)), dma((8,)), dma((group, ens_n)),
         ],
         compiler_params=pltpu.CompilerParams(
-            collective_id=0, has_side_effects=True, vmem_limit_bytes=48 * 1024 * 1024
+            collective_id=0, has_side_effects=True, vmem_limit_bytes=62 * 1024 * 1024
         ),
         cost_estimate=pl.CostEstimate(
             flops=cells * members * members * 6, bytes_accessed=cells * members * 8,

time: 108 us -> 102 us (0.944)
  local copies, waits for them, and re-layouts: 7.54 us -> 3.76 us
  Pallas kernels: 99.8 us -> 98.2 us
    unnamed x11 -> x1, local copies, waits for them, and re-layouts: 6.79 us -> 3.76 us
    pallas_call x1, Pallas kernels: 99.8 us -> 98.2 us  [body(): pl.pallas_call(functools.partial(kernel, dims), out_shape=jax.ShapeDtypeS...]
where the time goes in v3:
time: 102 us
  Pallas kernels  98.2 us (96%)
  local copies, waits for them, and re-layouts  3.76 us (4%)
    pallas_call x1, Pallas kernels, body(): pl.pallas_call(functools.partial(kernel, dims), out_shape=jax.ShapeDtypeS...  98.2 us
    unnamed x1, local copies, waits for them, and re-layouts  3.76 us

profile of v3, /device:TPU:11, one launch (start us, length us, event | category | flops | bytes accessed | tf_op | source)
XLA Modules:
  0.0 102.0 jit_solution(4402672866206143635)
XLA Ops:
  0.0 98.2 %shard_map.73 = f32[4,16,8,1440]{3,2,1,0:T(8,128)} custom-call(f32[4,16,8,1440]{3,2,1,0:T(8,128)} %in_ref.1, f32[4,8,1440]{2,1,0:T(8,128)} %obs_hbm.1, f32[16]{0:T(128)} %factor_ref.1, f32[8,8,128]{2,1,0:T(8,128)} %constant.11.clone.weight_hbm, bf16[4,256,256]{2,1,0:T(8,128)(2,1)} %constant.8.clone.band_hbm, bf16[4,256,256]{2,1,0:T(8,128)(2,1)} %constant.9.clone.back_hbm, ...), custom_call_target="tpu_custom_call" | custom-call | flops 75497472 | bytes 6291456 | tf_op jit(solution)/shard_map/pallas_call | solution.py:525
  98.2 3.8 %copy.9 = f32[4,16,8,1440]{3,2,1,0:T(8,128)} copy(f32[4,16,8,1440]{3,2,1,0:T(8,128)} %shard_map.73) | data formatting | bytes 5898240

commit v4 on v3

--- a/solution.py
+++ b/solution.py
@@ -11,6 +11,8 @@
 
 COARSE = 3
 LANES = 128
+COPIES = 4
+GRANT = 62 * 1024 * 1024
 MESH = pl.DeviceIdType.MESH
 
 
@@ -160,14 +162,6 @@
         for p in range(group // 2):
             obs_fields[obs_at + p] = jnp.zeros((rows, padded), jnp.float32)
 
-    @pl.when(jnp.logical_not(has_low))
-    def _():
-        zero_edges(True)
-
-    @pl.when(jnp.logical_not(has_high))
-    def _():
-        zero_edges(False)
-
     pl.semaphore_wait(barrier, ens_n - 1 + has_low.astype(jnp.int32) + has_high.astype(jnp.int32))
 
     def f_main(k, shift):
@@ -179,11 +173,11 @@
             device_id={"ens": target}, device_id_type=MESH,
         )
 
-    def f_rest(k, shift):
+    def f_rest(shift):
         target = peer(shift)
         return pltpu.make_async_remote_copy(
-            src_ref=rest_out.at[k, target], dst_ref=rests.at[k, me],
-            send_sem=fr_send.at[k, shift], recv_sem=fr_recv.at[k, shift],
+            src_ref=rest_out.at[target], dst_ref=rests.at[me],
+            send_sem=fr_send.at[shift], recv_sem=fr_recv.at[shift],
             device_id={"ens": target}, device_id_type=MESH,
         )
 
@@ -207,23 +201,33 @@
             total = jnp.where(lane < m * rest, total, pltpu.roll(tiles[m], m * rest, 1))
         return total
 
-    def start_rest(k):
-        for target in range(ens_n):
-            tile = packed([
+    def pack_rest(target, carry):
+        for k in range(group):
+            rest_out[target, k] = packed([
                 jnp.concatenate(
                     [staged[m, target * group + k, :, pl.ds(full, rest)],
                      jnp.zeros((rows, LANES - rest), jnp.float32)], axis=1)
                 for m in range(local)
             ])
-            rest_out[k, target] = tile
-        rests[k, me] = rest_out[k, me]
-        for shift in range(1, ens_n):
-            f_rest(k, shift).start()
+        return carry
 
     ahead = min(2, group)
     start_main(0)
+
+    @pl.when(jnp.logical_not(has_low))
+    def _():
+        zero_edges(True)
+
+    @pl.when(jnp.logical_not(has_high))
+    def _():
+        zero_edges(False)
+
     stage.wait()
-    start_rest(0)
+    lax.fori_loop(0, ens_n, pack_rest, 0)
+    rests[me] = rest_out[me]
+    for shift in range(1, ens_n):
+        f_rest(shift).start()
+
     upper = lax.broadcasted_iota(jnp.int32, (rows, padded), 0) < half
 
     def turn(tile):
@@ -303,16 +307,14 @@
     lon_blur(obs_sm, group, width)
     for k in range(1, ahead):
         start_main(k)
-        start_rest(k)
 
     def take_fields(k):
         for shift in range(1, ens_n):
             f_main(k, shift).wait_recv()
-            f_rest(k, shift).wait_recv()
         f_own(k).wait()
 
         def unpack(source, carry):
-            tile = rests[k, source]
+            tile = rests[source, k]
             for m in range(local):
                 fields[k, source * local + m, :, pl.ds(full, LANES)] = (
                     pltpu.roll(tile, LANES - m * rest, 1) if m else tile
@@ -333,7 +335,6 @@
         @pl.when(k + ahead < group)
         def _():
             start_main(k + ahead)
-            start_rest(k + ahead)
 
     block = 2 * LANES if padded % (2 * LANES) == 0 else LANES
 
@@ -348,6 +349,8 @@
 
         lax.fori_loop(0, padded // block, smooth_block, 0, unroll=3 if padded // block % 3 == 0 else 1)
         lon_blur(smooth, members, width)
+
+    def interact(k):
         weight = factor_ref[me * group + k] * jnp.broadcast_to(weight_ref[:, :1], (rows, LANES))
         pull = 0.95 / (members - 1)
         tiles = padded // LANES
@@ -394,11 +397,11 @@
             device_id={"ens": target}, device_id_type=MESH,
         )
 
-    def b_rest(k, shift):
+    def b_rest(shift):
         target = peer(shift)
         return pltpu.make_async_remote_copy(
-            src_ref=result_rest.at[k, target], dst_ref=rest_ref.at[me * group + k],
-            send_sem=br_send.at[k, shift], recv_sem=br_recv.at[k, shift],
+            src_ref=result_rest.at[target], dst_ref=rest_ref.at[pl.ds(me * group, group)],
+            send_sem=br_send.at[shift], recv_sem=br_recv.at[shift],
             device_id={"ens": target}, device_id_type=MESH,
         )
 
@@ -426,7 +429,7 @@
         lax.fori_loop(0, pairs, add, 0, unroll=4 if pairs % 4 == 0 else 1)
 
         def pack(target, carry):
-            result_rest[k, target] = packed(
+            result_rest[target, k] = packed(
                 [result[k, target * local + m, :, pl.ds(full, LANES)] for m in range(local)]
             )
             return carry
@@ -434,22 +437,24 @@
         lax.fori_loop(0, ens_n, pack, 0, unroll=True)
         for shift in range(1, ens_n):
             b_main(k, shift).start()
-            b_rest(k, shift).start()
         b_own(k).start()
-        rest_ref[me * group + k] = result_rest[k, me]
-
+
+    for shift in range(1, ens_n):
+        f_rest(shift).wait_recv()
     take_fields(0)
 
     def turn_of(k, carry):
         forward(k)
 
+        @pl.when(k + 1 < group)
+        def _():
+            take_fields(k + 1)
+
+        interact(k)
+
         @pl.when(k > 0)
         def _():
             finish(k - 1)
-
-        @pl.when(k + 1 < group)
-        def _():
-            take_fields(k + 1)
 
         backward(k)
 
@@ -457,13 +462,27 @@
 
     lax.fori_loop(0, group, turn_of, 0)
     finish(group - 1)
+    for shift in range(1, ens_n):
+        b_rest(shift).start()
+    rest_ref[pl.ds(me * group, group)] = result_rest[me]
 
     sent_both(obs_copies)
 
     def drain(k, carry):
         for shift in range(1, ens_n):
-            b_main(k, shift).wait_recv()
-            b_rest(k, shift).wait_recv()
+            f_main(k, shift).wait_send()
+        sent_both(halo_copies(k))
+        sent_both(edge_copies(k))
+        return carry
+
+    lax.fori_loop(0, group, drain, 0)
+    for shift in range(1, ens_n):
+        f_rest(shift).wait_send()
+        b_rest(shift).wait()
+
+    def collect(k, carry):
+        for shift in range(1, ens_n):
+            b_main(k, shift).wait()
         b_own(k).wait()
 
         def unpack(source, inner):
@@ -474,17 +493,10 @@
             write(k, source).start()
             return inner
 
-        lax.fori_loop(0, ens_n, unpack, 0)
-        for shift in range(1, ens_n):
-            f_main(k, shift).wait_send()
-            f_rest(k, shift).wait_send()
-            b_main(k, shift).wait_send()
-            b_rest(k, shift).wait_send()
-        sent_both(halo_copies(k))
-        sent_both(edge_copies(k))
+        lax.fori_loop(0, ens_n, unpack, 0, unroll=True)
         return carry
 
-    lax.fori_loop(0, group, drain, 0)
+    lax.fori_loop(0, group, collect, 0)
 
     def close(k, carry):
         for source in range(ens_n):
@@ -492,6 +504,22 @@
         return carry
 
     lax.fori_loop(0, group, close, 0)
+
+
+def pass_on(in_ref, out_ref, sem):
+    local, channels = in_ref.shape[:2]
+    size = channels // COPIES
+    copies = [
+        pltpu.make_async_copy(
+            in_ref.at[m, pl.ds(part * size, size)], out_ref.at[m, pl.ds(part * size, size)], sem.at[m, part]
+        )
+        for m in range(local)
+        for part in range(COPIES)
+    ]
+    for copy in copies:
+        copy.start()
+    for copy in copies:
+        copy.wait()
 
 
 def body(prediction_array, verifying_analysis, variable_penalty_factor):
@@ -518,15 +546,15 @@
     weights = jnp.asarray(np.pad(weights, ((0, 0), (0, 0), (0, LANES - 1))))
 
     dims = (ens_n, lat_n, local, members, group, rows, width)
-    hbm = pl.BlockSpec(memory_space=pl.ANY)
+    hbm = pl.BlockSpec(memory_space=pltpu.HBM)
     f32 = jnp.float32
     dma = pltpu.SemaphoreType.DMA
     cells = group * padded * rows
-    return pl.pallas_call(
+    gathered = pl.pallas_call(
         functools.partial(kernel, dims),
         out_shape=jax.ShapeDtypeStruct((local, channels, rows, width), f32),
         in_specs=[hbm, hbm, pl.BlockSpec(memory_space=pltpu.SMEM), hbm, hbm, hbm, hbm],
-        out_specs=hbm,
+        out_specs=pl.BlockSpec(memory_space=pl.ANY),
         scratch_shapes=[
             pltpu.VMEM((local, channels, rows, width), f32),
             pltpu.VMEM((channels, rows, LANES), f32),
@@ -537,31 +565,39 @@
             pltpu.VMEM(obs_band.shape[1:], jnp.bfloat16),
             pltpu.VMEM((local, channels, rows, width), f32),
             pltpu.VMEM((group, members + 2 * pairs, rows, padded), f32),
-            pltpu.VMEM((group, ens_n, rows, LANES), f32),
-            pltpu.VMEM((group, ens_n, rows, LANES), f32),
+            pltpu.VMEM((ens_n, group, rows, LANES), f32),
+            pltpu.VMEM((ens_n, group, rows, LANES), f32),
             pltpu.VMEM((group, 2, pairs, rows, padded), f32),
             pltpu.VMEM((2 * group, rows, padded), f32),
             pltpu.VMEM((2, group // 2, rows, padded), f32),
             pltpu.VMEM((2 * group, rows, padded), f32),
             pltpu.VMEM((2 * members, rows, padded), f32),
             pltpu.VMEM((group, members, rows, padded), f32),
-            pltpu.VMEM((group, ens_n, rows, LANES), f32),
+            pltpu.VMEM((ens_n, group, rows, LANES), f32),
             pltpu.VMEM((group, 2, pairs, rows, padded), f32),
             pltpu.VMEM((group, 2, pairs, rows, padded), f32),
-            dma((group, ens_n)), dma((group, ens_n)), dma((group, ens_n)), dma((group, ens_n)),
+            dma((group, ens_n)), dma((group, ens_n)), dma((ens_n,)), dma((ens_n,)),
             dma((group,)), dma,
             dma((group, 2)), dma((group, 2)), dma((2,)), dma((2,)), dma((group, 2)), dma((group, 2)),
-            dma((group, ens_n)), dma((group, ens_n)), dma((group, ens_n)), dma((group, ens_n)),
+            dma((group, ens_n)), dma((group, ens_n)), dma((ens_n,)), dma((ens_n,)),
             dma((group,)), dma((8,)), dma((group, ens_n)),
         ],
         compiler_params=pltpu.CompilerParams(
-            collective_id=0, has_side_effects=True, vmem_limit_bytes=62 * 1024 * 1024
+            collective_id=0, has_side_effects=True, vmem_limit_bytes=GRANT
         ),
         cost_estimate=pl.CostEstimate(
             flops=cells * members * members * 6, bytes_accessed=cells * members * 8,
             transcendentals=cells * members * members,
         ),
     )(prediction_array, verifying_analysis, variable_penalty_factor, weights, band, back, obs_band)
+    return pl.pallas_call(
+        pass_on,
+        out_shape=jax.ShapeDtypeStruct(gathered.shape, f32),
+        in_specs=[hbm],
+        out_specs=hbm,
+        scratch_shapes=[dma((local, COPIES))],
+        compiler_params=pltpu.CompilerParams(vmem_limit_bytes=GRANT),
+    )(gathered)
 
 
 def solution(mesh):

time: 102 us -> 191 us (1.87)
  Pallas kernels: 98.2 us -> 190 us
  local copies, waits for them, and re-layouts: 3.76 us -> 0 us
    pallas_call x0 -> x1, Pallas kernels: none -> 96.5 us  [body(): pl.pallas_call(pass_on, out_shape=jax.ShapeDtypeStruct(gathered.shape, f3...]
    pallas_call x1, Pallas kernels: 98.2 us -> 93.3 us  [body(): pl.pallas_call(functools.partial(kernel, dims), out_shape=jax.ShapeDtypeS...]
    unnamed x1 -> x0, local copies, waits for them, and re-layouts: 3.76 us -> none
where the time goes in v4:
time: 191 us; the launch traced here: 190 us
  Pallas kernels  190 us (99%)
    pallas_call x1, Pallas kernels, body(): pl.pallas_call(pass_on, out_shape=jax.ShapeDtypeStruct(gathered.shape, f3...  96.5 us
    pallas_call x1, Pallas kernels, body(): pl.pallas_call(functools.partial(kernel, dims), out_shape=jax.ShapeDtypeS...  93.3 us

profile of v4, /device:TPU:11, one launch (start us, length us, event | category | flops | bytes accessed | tf_op | source)
XLA Modules:
  0.0 189.8 jit_solution(836698298993981672)
XLA Ops:
  0.0 93.3 %shard_map.73.in_ref = f32[4,16,8,1440]{3,2,1,0:T(8,128)} custom-call(f32[4,16,8,1440]{3,2,1,0:T(8,128)} %in_ref.1, f32[4,8,1440]{2,1,0:T(8,128)} %obs_hbm.1, f32[16]{0:T(128)} %factor_ref.1, f32[8,8,128]{2,1,0:T(8,128)} %constant.11.clone.weight_hbm, bf16[4,256,256]{2,1,0:T(8,128)(2,1)} %constant.8.clone.band_hbm, ...), custom_call_target="tpu_custom_call" | custom-call | flops 75497472 | bytes 6291456 | tf_op jit(solution)/shard_map/pallas_call | solution.py:553
  93.3 96.5 %shard_map.74 = f32[4,16,8,1440]{3,2,1,0:T(8,128)} custom-call(f32[4,16,8,1440]{3,2,1,0:T(8,128)} %shard_map.73.in_ref), custom_call_target="tpu_custom_call" | custom-call | tf_op jit(solution)/shard_map/pallas_call | solution.py:593

commit v5 on v4

--- a/solution.py
+++ b/solution.py
@@ -108,6 +108,10 @@
     rest = width - full
     padded = full + LANES
     total_rows = 2 * members * rows
+    block = 2 * LANES if padded % (2 * LANES) == 0 else LANES
+    cut = (padded // block + 1) // 2 * block
+    ranges = ((0, cut), (cut, padded))
+    last = len(ranges) - 1
     me = lax.axis_index("ens")
     lat = lax.axis_index("lat")
     has_low = lat > 0
@@ -164,12 +168,16 @@
 
     pl.semaphore_wait(barrier, ens_n - 1 + has_low.astype(jnp.int32) + has_high.astype(jnp.int32))
 
-    def f_main(k, shift):
+    def sent_lanes(h):
+        low, high = ranges[h]
+        return pl.ds(low, min(high, full) - low)
+
+    def f_main(k, h, shift):
         target = peer(shift)
         return pltpu.make_async_remote_copy(
-            src_ref=in_ref.at[:, target * group + k, :, pl.ds(0, full)],
-            dst_ref=fields.at[k, pl.ds(me * local, local), :, pl.ds(0, full)],
-            send_sem=f_send.at[k, shift], recv_sem=f_recv.at[k, shift],
+            src_ref=in_ref.at[:, target * group + k, :, sent_lanes(h)],
+            dst_ref=fields.at[k, pl.ds(me * local, local), :, sent_lanes(h)],
+            send_sem=f_send.at[k, h, shift], recv_sem=f_recv.at[k, h, shift],
             device_id={"ens": target}, device_id_type=MESH,
         )
 
@@ -189,8 +197,9 @@
         )
 
     def start_main(k):
-        for shift in range(1, ens_n):
-            f_main(k, shift).start()
+        for h in range(len(ranges)):
+            for shift in range(1, ens_n):
+                f_main(k, h, shift).start()
         f_own(k).start()
 
     lane = lax.broadcasted_iota(jnp.int32, (rows, LANES), 1)
@@ -228,7 +237,8 @@
     for shift in range(1, ens_n):
         f_rest(shift).start()
 
-    upper = lax.broadcasted_iota(jnp.int32, (rows, padded), 0) < half
+    def upper(size):
+        return lax.broadcasted_iota(jnp.int32, (rows, size), 0) < half
 
     def turn(tile):
         return pltpu.roll(tile, half, 0)
@@ -272,17 +282,22 @@
         def _():
             copies[1].wait_send()
 
-    def halo_copies(k):
+    def lanes(h):
+        return pl.ds(ranges[h][0], ranges[h][1] - ranges[h][0])
+
+    def halo_copies(k, h):
         return neighbour_copies(
-            (halo_out.at[k, 0], halo_out.at[k, 1]),
-            (fields.at[k, pl.ds(members, pairs)], fields.at[k, pl.ds(members + pairs, pairs)]),
-            h_send.at[k], h_recv.at[k],
-        )
-
-    def edge_copies(k):
+            (halo_out.at[k, 0, :, :, lanes(h)], halo_out.at[k, 1, :, :, lanes(h)]),
+            (fields.at[k, pl.ds(members, pairs), :, lanes(h)],
+             fields.at[k, pl.ds(members + pairs, pairs), :, lanes(h)]),
+            h_send.at[k, h], h_recv.at[k, h],
+        )
+
+    def edge_copies(k, h):
         return neighbour_copies(
-            (edge_out.at[k, 0], edge_out.at[k, 1]), (edge_in.at[k, 0], edge_in.at[k, 1]),
-            e_send.at[k], e_recv.at[k],
+            (edge_out.at[k, 0, :, :, lanes(h)], edge_out.at[k, 1, :, :, lanes(h)]),
+            (edge_in.at[k, 0, :, :, lanes(h)], edge_in.at[k, 1, :, :, lanes(h)]),
+            e_send.at[k, h], e_recv.at[k, h],
         )
 
     for load in loads:
@@ -298,8 +313,8 @@
         obs_fields[c, :, pl.ds(0, width)] = obs_ref[c]
     for p in range(couples):
         one, two = obs_fields[p], obs_fields[p + couples]
-        obs_halo[0, p] = jnp.where(upper, one, turn(two))
-        obs_halo[1, p] = jnp.where(upper, turn(one), two)
+        obs_halo[0, p] = jnp.where(upper(padded), one, turn(two))
+        obs_halo[1, p] = jnp.where(upper(padded), turn(one), two)
     start_both(obs_copies)
     recv_both(obs_copies)
     values = obs_fields[...].reshape(2 * group * rows, padded)
@@ -309,45 +324,47 @@
         start_main(k)
 
     def take_fields(k):
-        for shift in range(1, ens_n):
-            f_main(k, shift).wait_recv()
         f_own(k).wait()
-
-        def unpack(source, carry):
-            tile = rests[source, k]
-            for m in range(local):
-                fields[k, source * local + m, :, pl.ds(full, LANES)] = (
-                    pltpu.roll(tile, LANES - m * rest, 1) if m else tile
-                )
-            return carry
-
-        lax.fori_loop(0, ens_n, unpack, 0, unroll=True)
-
-        def pack_halo(p, carry):
-            one, two = fields[k, p], fields[k, p + pairs]
-            halo_out[k, 0, p] = jnp.where(upper, one, turn(two))
-            halo_out[k, 1, p] = jnp.where(upper, turn(one), two)
-            return carry
-
-        lax.fori_loop(0, pairs, pack_halo, 0, unroll=4 if pairs % 4 == 0 else 1)
-        start_both(halo_copies(k))
+        for h in range(len(ranges)):
+            for shift in range(1, ens_n):
+                f_main(k, h, shift).wait_recv()
+
+            if h == last:
+                def unpack(source, carry):
+                    tile = rests[source, k]
+                    for m in range(local):
+                        fields[k, source * local + m, :, pl.ds(full, LANES)] = (
+                            pltpu.roll(tile, LANES - m * rest, 1) if m else tile
+                        )
+                    return carry
+
+                lax.fori_loop(0, ens_n, unpack, 0, unroll=True)
+
+            def pack_halo(p, carry):
+                one, two = fields[k, p, :, lanes(h)], fields[k, p + pairs, :, lanes(h)]
+                mask = upper(one.shape[1])
+                halo_out[k, 0, p, :, lanes(h)] = jnp.where(mask, one, turn(two))
+                halo_out[k, 1, p, :, lanes(h)] = jnp.where(mask, turn(one), two)
+                return carry
+
+            lax.fori_loop(0, pairs, pack_halo, 0, unroll=4 if pairs % 4 == 0 else 1)
+            start_both(halo_copies(k, h))
 
         @pl.when(k + ahead < group)
         def _():
             start_main(k + ahead)
 
-    block = 2 * LANES if padded % (2 * LANES) == 0 else LANES
 
     def forward(k):
-        recv_both(halo_copies(k))
-
         def smooth_block(b, carry):
             at = pl.ds(pl.multiple_of(b * block, block), block)
             values = fields[k, :, :, at].reshape(total_rows, block)
             smooth[:, :, at] = split_dot(band_ref[...], values, 3).reshape(2 * members, rows, block)
             return carry
 
-        lax.fori_loop(0, padded // block, smooth_block, 0, unroll=3 if padded // block % 3 == 0 else 1)
+        for h, (low, high) in enumerate(ranges):
+            recv_both(halo_copies(k, h))
+            lax.fori_loop(low // block, high // block, smooth_block, 0, unroll=True)
         lon_blur(smooth, members, width)
 
     def interact(k):
@@ -385,15 +402,16 @@
             edge_out[k, 1, :, :, at] = out[members + pairs :]
             return carry
 
-        lax.fori_loop(0, padded // block, back_block, 0, unroll=3 if padded // block % 3 == 0 else 1)
-        start_both(edge_copies(k))
-
-    def b_main(k, shift):
+        for h, (low, high) in enumerate(ranges):
+            lax.fori_loop(low // block, high // block, back_block, 0, unroll=True)
+            start_both(edge_copies(k, h))
+
+    def b_main(k, h, shift):
         target = peer(shift)
         return pltpu.make_async_remote_copy(
-            src_ref=result.at[k, pl.ds(target * local, local), :, pl.ds(0, full)],
-            dst_ref=main_ref.at[:, me * group + k, :, pl.ds(0, full)],
-            send_sem=b_send.at[k, shift], recv_sem=b_recv.at[k, shift],
+            src_ref=result.at[k, pl.ds(target * local, local), :, sent_lanes(h)],
+            dst_ref=main_ref.at[:, me * group + k, :, sent_lanes(h)],
+            send_sem=b_send.at[k, h, shift], recv_sem=b_recv.at[k, h, shift],
             device_id={"ens": target}, device_id_type=MESH,
         )
 
@@ -418,15 +436,20 @@
         )
 
     def finish(k):
-        recv_both(edge_copies(k))
-
-        def add(p, carry):
-            low, high = edge_in[k, 0, p], edge_in[k, 1, p]
-            result[k, p] = result[k, p] + jnp.where(upper, low, turn(high))
-            result[k, p + pairs] = result[k, p + pairs] + jnp.where(upper, turn(low), high)
-            return carry
-
-        lax.fori_loop(0, pairs, add, 0, unroll=4 if pairs % 4 == 0 else 1)
+        for h in range(len(ranges)):
+            recv_both(edge_copies(k, h))
+
+            def add(p, carry):
+                low, high = edge_in[k, 0, p, :, lanes(h)], edge_in[k, 1, p, :, lanes(h)]
+                mask = upper(low.shape[1])
+                one, two = result[k, p, :, lanes(h)], result[k, p + pairs, :, lanes(h)]
+                result[k, p, :, lanes(h)] = one + jnp.where(mask, low, turn(high))
+                result[k, p + pairs, :, lanes(h)] = two + jnp.where(mask, turn(low), high)
+                return carry
+
+            lax.fori_loop(0, pairs, add, 0, unroll=4 if pairs % 4 == 0 else 1)
+            for shift in range(1, ens_n):
+                b_main(k, h, shift).start()
 
         def pack(target, carry):
             result_rest[target, k] = packed(
@@ -435,8 +458,6 @@
             return carry
 
         lax.fori_loop(0, ens_n, pack, 0, unroll=True)
-        for shift in range(1, ens_n):
-            b_main(k, shift).start()
         b_own(k).start()
 
     for shift in range(1, ens_n):
@@ -469,10 +490,11 @@
     sent_both(obs_copies)
 
     def drain(k, carry):
-        for shift in range(1, ens_n):
-            f_main(k, shift).wait_send()
-        sent_both(halo_copies(k))
-        sent_both(edge_copies(k))
+        for h in range(len(ranges)):
+            for shift in range(1, ens_n):
+                f_main(k, h, shift).wait_send()
+            sent_both(halo_copies(k, h))
+            sent_both(edge_copies(k, h))
         return carry
 
     lax.fori_loop(0, group, drain, 0)
@@ -481,8 +503,9 @@
         b_rest(shift).wait()
 
     def collect(k, carry):
-        for shift in range(1, ens_n):
-            b_main(k, shift).wait()
+        for h in range(len(ranges)):
+            for shift in range(1, ens_n):
+                b_main(k, h, shift).wait()
         b_own(k).wait()
 
         def unpack(source, inner):
@@ -506,20 +529,19 @@
     lax.fori_loop(0, group, close, 0)
 
 
-def pass_on(in_ref, out_ref, sem):
+def pass_on(in_ref, out_ref, held, in_sem, out_sem):
     local, channels = in_ref.shape[:2]
     size = channels // COPIES
-    copies = [
-        pltpu.make_async_copy(
-            in_ref.at[m, pl.ds(part * size, size)], out_ref.at[m, pl.ds(part * size, size)], sem.at[m, part]
-        )
-        for m in range(local)
-        for part in range(COPIES)
-    ]
-    for copy in copies:
-        copy.start()
-    for copy in copies:
-        copy.wait()
+    parts = [(m, pl.ds(part * size, size)) for m in range(local) for part in range(COPIES)]
+    reads = [pltpu.make_async_copy(in_ref.at[at], held.at[at], in_sem.at[i]) for i, at in enumerate(parts)]
+    writes = [pltpu.make_async_copy(held.at[at], out_ref.at[at], out_sem.at[i]) for i, at in enumerate(parts)]
+    for read in reads:
+        read.start()
+    for read, write in zip(reads, writes):
+        read.wait()
+        write.start()
+    for write in writes:
+        write.wait()
 
 
 def body(prediction_array, verifying_analysis, variable_penalty_factor):
@@ -576,10 +598,10 @@
             pltpu.VMEM((ens_n, group, rows, LANES), f32),
             pltpu.VMEM((group, 2, pairs, rows, padded), f32),
             pltpu.VMEM((group, 2, pairs, rows, padded), f32),
-            dma((group, ens_n)), dma((group, ens_n)), dma((ens_n,)), dma((ens_n,)),
+            dma((group, 2, ens_n)), dma((group, 2, ens_n)), dma((ens_n,)), dma((ens_n,)),
             dma((group,)), dma,
-            dma((group, 2)), dma((group, 2)), dma((2,)), dma((2,)), dma((group, 2)), dma((group, 2)),
-            dma((group, ens_n)), dma((group, ens_n)), dma((ens_n,)), dma((ens_n,)),
+            dma((group, 2, 2)), dma((group, 2, 2)), dma((2,)), dma((2,)), dma((group, 2, 2)), dma((group, 2, 2)),
+            dma((group, 2, ens_n)), dma((group, 2, ens_n)), dma((ens_n,)), dma((ens_n,)),
             dma((group,)), dma((8,)), dma((group, ens_n)),
         ],
         compiler_params=pltpu.CompilerParams(
@@ -595,7 +617,7 @@
         out_shape=jax.ShapeDtypeStruct(gathered.shape, f32),
         in_specs=[hbm],
         out_specs=hbm,
-        scratch_shapes=[dma((local, COPIES))],
+        scratch_shapes=[pltpu.VMEM(gathered.shape, f32), dma((local * COPIES,)), dma((local * COPIES,))],
         compiler_params=pltpu.CompilerParams(vmem_limit_bytes=GRANT),
     )(gathered)
 

time: 191 us -> 93.8 us (0.49)
  Pallas kernels: 190 us -> 92 us
    pallas_call x1, Pallas kernels: 96.5 us -> 3.17 us  [body(): pl.pallas_call(pass_on, out_shape=jax.ShapeDtypeStruct(gathered.shape, f3...]
    pallas_call x1, Pallas kernels: 93.3 us -> 88.8 us  [body(): pl.pallas_call(functools.partial(kernel, dims), out_shape=jax.ShapeDtypeS...]
where the time goes in v5:
time: 93.8 us; the launch traced here: 92 us
  Pallas kernels  92 us (98%)
    pallas_call x1, Pallas kernels, body(): pl.pallas_call(functools.partial(kernel, dims), out_shape=jax.ShapeDtypeS...  88.8 us
    pallas_call x1, Pallas kernels, body(): pl.pallas_call(pass_on, out_shape=jax.ShapeDtypeStruct(gathered.shape, f3...  3.17 us

profile of v5, /device:TPU:11, one launch (start us, length us, event | category | flops | bytes accessed | tf_op | source)
XLA Modules:
  0.0 92.0 jit_solution(7701092190894239961)
XLA Ops:
  0.0 88.8 %shard_map.73.in_ref = f32[4,16,8,1440]{3,2,1,0:T(8,128)} custom-call(f32[4,16,8,1440]{3,2,1,0:T(8,128)} %in_ref.1, f32[4,8,1440]{2,1,0:T(8,128)} %obs_hbm.1, f32[16]{0:T(128)} %factor_ref.1, f32[8,8,128]{2,1,0:T(8,128)} %constant.11.clone.weight_hbm, bf16[4,256,256]{2,1,0:T(8,128)(2,1)} %constant.8.clone.band_hbm, ...), custom_call_target="tpu_custom_call" | custom-call | flops 75497472 | bytes 6291456 | tf_op jit(solution)/shard_map/pallas_call | solution.py:575
  88.9 3.2 %shard_map.74 = f32[4,16,8,1440]{3,2,1,0:T(8,128)} custom-call(f32[4,16,8,1440]{3,2,1,0:T(8,128)} %shard_map.73.in_ref), custom_call_target="tpu_custom_call" | custom-call | tf_op jit(solution)/shard_map/pallas_call | solution.py:615

commit v6 on v5

--- a/solution.py
+++ b/solution.py
@@ -220,7 +220,6 @@
             ])
         return carry
 
-    ahead = min(2, group)
     start_main(0)
 
     @pl.when(jnp.logical_not(has_low))
@@ -320,8 +319,6 @@
     values = obs_fields[...].reshape(2 * group * rows, padded)
     obs_sm[...] = split_dot(obs_band_ref[...], values, 3).reshape(2 * group, rows, padded)
     lon_blur(obs_sm, group, width)
-    for k in range(1, ahead):
-        start_main(k)
 
     def take_fields(k):
         f_own(k).wait()
@@ -330,6 +327,10 @@
                 f_main(k, h, shift).wait_recv()
 
             if h == last:
+                @pl.when(k + 1 < group)
+                def _():
+                    start_main(k + 1)
+
                 def unpack(source, carry):
                     tile = rests[source, k]
                     for m in range(local):
@@ -349,11 +350,6 @@
 
             lax.fori_loop(0, pairs, pack_halo, 0, unroll=4 if pairs % 4 == 0 else 1)
             start_both(halo_copies(k, h))
-
-        @pl.when(k + ahead < group)
-        def _():
-            start_main(k + ahead)
-
 
     def forward(k):
         def smooth_block(b, carry):

time: 93.8 us -> 93.7 us (level)
  no operation moved by 1% of the time
where the time goes in v6:
time: 93.7 us; the launch traced here: 92.7 us
  Pallas kernels  92.6 us (99%)
    pallas_call x1, Pallas kernels, body(): pl.pallas_call(functools.partial(kernel, dims), out_shape=jax.ShapeDtypeS...  89.5 us
    pallas_call x1, Pallas kernels, body(): pl.pallas_call(pass_on, out_shape=jax.ShapeDtypeStruct(gathered.shape, f3...  3.17 us

profile of v6, /device:TPU:11, one launch (start us, length us, event | category | flops | bytes accessed | tf_op | source)
XLA Modules:
  0.0 92.7 jit_solution(9781871059803787276)
XLA Ops:
  0.0 89.5 %shard_map.73.in_ref = f32[4,16,8,1440]{3,2,1,0:T(8,128)} custom-call(f32[4,16,8,1440]{3,2,1,0:T(8,128)} %in_ref.1, f32[4,8,1440]{2,1,0:T(8,128)} %obs_hbm.1, f32[16]{0:T(128)} %factor_ref.1, f32[8,8,128]{2,1,0:T(8,128)} %constant.11.clone.weight_hbm, bf16[4,256,256]{2,1,0:T(8,128)(2,1)} %constant.8.clone.band_hbm, ...), custom_call_target="tpu_custom_call" | custom-call | flops 75497472 | bytes 6291456 | tf_op jit(solution)/shard_map/pallas_call | solution.py:571
  89.5 3.2 %shard_map.74 = f32[4,16,8,1440]{3,2,1,0:T(8,128)} custom-call(f32[4,16,8,1440]{3,2,1,0:T(8,128)} %shard_map.73.in_ref), custom_call_target="tpu_custom_call" | custom-call | tf_op jit(solution)/shard_map/pallas_call | solution.py:611

commit v7 on v6

--- a/solution.py
+++ b/solution.py
@@ -327,10 +327,6 @@
                 f_main(k, h, shift).wait_recv()
 
             if h == last:
-                @pl.when(k + 1 < group)
-                def _():
-                    start_main(k + 1)
-
                 def unpack(source, carry):
                     tile = rests[source, k]
                     for m in range(local):
@@ -350,6 +346,10 @@
 
             lax.fori_loop(0, pairs, pack_halo, 0, unroll=4 if pairs % 4 == 0 else 1)
             start_both(halo_copies(k, h))
+
+        @pl.when(k + 1 < group)
+        def _():
+            start_main(k + 1)
 
     def forward(k):
         def smooth_block(b, carry):
@@ -469,11 +469,12 @@
 
         interact(k)
 
+        backward(k)
+
         @pl.when(k > 0)
         def _():
             finish(k - 1)
 
-        backward(k)
 
         return carry
 

time: 93.7 us -> 97.9 us (1.045)
  Pallas kernels: 92.6 us -> 96.1 us
    pallas_call x1, Pallas kernels: 89.5 us -> 92.9 us  [body(): pl.pallas_call(functools.partial(kernel, dims), out_shape=jax.ShapeDtypeS...]
where the time goes in v7:
time: 97.9 us; the launch traced here: 96.1 us
  Pallas kernels  96.1 us (98%)
    pallas_call x1, Pallas kernels, body(): pl.pallas_call(functools.partial(kernel, dims), out_shape=jax.ShapeDtypeS...  92.9 us
    pallas_call x1, Pallas kernels, body(): pl.pallas_call(pass_on, out_shape=jax.ShapeDtypeStruct(gathered.shape, f3...  3.17 us

profile of v7, /device:TPU:11, one launch (start us, length us, event | category | flops | bytes accessed | tf_op | source)
XLA Modules:
  0.0 96.1 jit_solution(11333350829868313952)
XLA Ops:
  0.0 92.9 %shard_map.73.in_ref = f32[4,16,8,1440]{3,2,1,0:T(8,128)} custom-call(f32[4,16,8,1440]{3,2,1,0:T(8,128)} %in_ref.1, f32[4,8,1440]{2,1,0:T(8,128)} %obs_hbm.1, f32[16]{0:T(128)} %factor_ref.1, f32[8,8,128]{2,1,0:T(8,128)} %constant.11.clone.weight_hbm, bf16[4,256,256]{2,1,0:T(8,128)(2,1)} %constant.8.clone.band_hbm, ...), custom_call_target="tpu_custom_call" | custom-call | flops 75497472 | bytes 6291456 | tf_op jit(solution)/shard_map/pallas_call | solution.py:572
  92.9 3.2 %shard_map.74 = f32[4,16,8,1440]{3,2,1,0:T(8,128)} custom-call(f32[4,16,8,1440]{3,2,1,0:T(8,128)} %shard_map.73.in_ref), custom_call_target="tpu_custom_call" | custom-call | tf_op jit(solution)/shard_map/pallas_call | solution.py:612

commit v8 on v7

--- a/solution.py
+++ b/solution.py
@@ -384,7 +384,7 @@
                 smooth[base + m, :, at] = weight * (slope(held[m] - analysis) - pull * sums[m])
             return carry
 
-        lax.fori_loop(0, 2 * tiles, couple, 0)
+        lax.fori_loop(0, 2 * tiles, couple, 0, unroll=2)
 
     def backward(k):
         lon_blur(smooth, members, width)
@@ -469,12 +469,11 @@
 
         interact(k)
 
+        @pl.when(k > 0)
+        def _():
+            finish(k - 1)
+
         backward(k)
-
-        @pl.when(k > 0)
-        def _():
-            finish(k - 1)
-
 
         return carry
 

time: 97.9 us -> 93.1 us (0.951)
  Pallas kernels: 96.1 us -> 92.2 us
    pallas_call x1, Pallas kernels: 92.9 us -> 89 us  [body(): pl.pallas_call(functools.partial(kernel, dims), out_shape=jax.ShapeDtypeS...]
where the time goes in v8:
time: 93.1 us; the launch traced here: 92.2 us
  Pallas kernels  92.2 us (99%)
    pallas_call x1, Pallas kernels, body(): pl.pallas_call(functools.partial(kernel, dims), out_shape=jax.ShapeDtypeS...  89 us
    pallas_call x1, Pallas kernels, body(): pl.pallas_call(pass_on, out_shape=jax.ShapeDtypeStruct(gathered.shape, f3...  3.17 us

profile of v8, /device:TPU:11, one launch (start us, length us, event | category | flops | bytes accessed | tf_op | source)
XLA Modules:
  0.0 92.2 jit_solution(14268120388994871771)
XLA Ops:
  0.0 89.0 %shard_map.73.in_ref = f32[4,16,8,1440]{3,2,1,0:T(8,128)} custom-call(f32[4,16,8,1440]{3,2,1,0:T(8,128)} %in_ref.1, f32[4,8,1440]{2,1,0:T(8,128)} %obs_hbm.1, f32[16]{0:T(128)} %factor_ref.1, f32[8,8,128]{2,1,0:T(8,128)} %constant.11.clone.weight_hbm, bf16[4,256,256]{2,1,0:T(8,128)(2,1)} %constant.8.clone.band_hbm, ...), custom_call_target="tpu_custom_call" | custom-call | flops 75497472 | bytes 6291456 | tf_op jit(solution)/shard_map/pallas_call | solution.py:571
  89.0 3.2 %shard_map.74 = f32[4,16,8,1440]{3,2,1,0:T(8,128)} custom-call(f32[4,16,8,1440]{3,2,1,0:T(8,128)} %shard_map.73.in_ref), custom_call_target="tpu_custom_call" | custom-call | tf_op jit(solution)/shard_map/pallas_call | solution.py:611
